TPU v7x, 32 devices: a whole 2x2x4 slice. The times are simulated.
32 devices in a mesh: fsdp: 2 (over x), heads: 4 (over z), tensor: 4 (over y, core).
Axes of the slice: x: 2, y: 2, z: 4, core: 2. Of those that a mesh axis runs over, the one named last changes fastest.
Arguments:
- tokens: bfloat16 [12608, 512], P(('fsdp', 'heads', 'tensor')), may hold values from -6 to 6
- gain_one: bfloat16 [512], P('fsdp'), may hold values from 0.5 to 1.5
- shift_one: bfloat16 [512], P('fsdp'), may hold values from -2 to 2
- w_qkv: bfloat16 [3, 512, 512], P(None, 'fsdp', 'heads'), may hold values from -0.25 to 0.25
- w_attn_out: bfloat16 [512, 512], P('heads', 'fsdp'), may hold values from -2 to 2
- gain_two: bfloat16 [512], P('fsdp'), may hold values from 0.5 to 1.5
- shift_two: bfloat16 [512], P('fsdp'), may hold values from -2 to 2
- w_router: bfloat16 [512, 4], P('fsdp'), may hold values from -0.26367188 to 0.26367188
- w_in: bfloat16 [4, 512, 2048], P(None, 'fsdp', 'tensor'), may hold values from -0.25 to 0.25
- w_out: bfloat16 [4, 2048, 512], P(None, 'tensor', 'fsdp'), may hold values from -0.375 to 0.375
- routes: int32 [12608, 2], P(('fsdp', 'heads')), may hold values from 0 to 3, all different within a row; in each aligned block of 394 rows (0 to 393, 394 to 787, ...) at most 246 rows name the same one
- cotangent: bfloat16 [12608, 512], P(('fsdp', 'heads', 'tensor')), may hold values from -6 to 6
Outputs:
- output: bfloat16 [12608, 512], P(('fsdp', 'heads', 'tensor'))
- input_grad: bfloat16 [12608, 512], P(('fsdp', 'heads', 'tensor'))
- gain_one_grad: float32 [512], P('fsdp')
- shift_one_grad: float32 [512], P('fsdp')
- w_qkv_grad: float32 [3, 512, 512], P(None, 'fsdp', 'heads')
- w_attn_out_grad: float32 [512, 512], P('heads', 'fsdp')
- gain_two_grad: float32 [512], P('fsdp')
- shift_two_grad: float32 [512], P('fsdp')
- w_router_grad: float32 [512, 4], P('fsdp')
- w_in_grad: float32 [4, 512, 2048], P(None, 'fsdp', 'tensor')
- w_out_grad: float32 [4, 2048, 512], P(None, 'tensor', 'fsdp')
Inputs may be any that keep to these rules, and one draw needn't show every extreme that they name: `routes`: the two experts of a row differ; in each aligned block of 394 rows (the rows of one device) no expert is named by more than 246 rows, and in some blocks one is named by exactly 246.
All inputs are finite; a program needn't handle non-finite values.
Results may differ from a plain program's by a relative error of at most 0.025.
Values may be sent and summed in bfloat16 or wider, within the bound.
No kernel may reach another device: no remote copies, remote signals or barrier semaphores. Data moves between devices by JAX's collectives and lax.ppermute only.
A program may use at most 128 MiB of HBM per device.

v0:
```python
import jax
import jax.numpy as jnp
from jax import lax
from jax.sharding import PartitionSpec as P

HD = 64
SEQ = 197
MOST = 246


def layer_norm(values, gain, shift):
    center = jnp.mean(values, -1, keepdims=True)
    centered = values - center
    spread = jnp.mean(centered * centered, -1, keepdims=True)
    return centered * lax.rsqrt(spread + 1e-06) * gain + shift


def local(
    tokens,
    gain_one,
    shift_one,
    w_qkv,
    w_attn_out,
    gain_two,
    shift_two,
    w_router,
    w_in,
    w_out,
    routes,
    cotangent,
):
    (
        gain_one_all,
        shift_one_all,
        qkv_full,
        attn_out_full,
        gain_two_all,
        shift_two_all,
        router_full,
        inner_full,
        outer_full,
    ) = (
        lax.all_gather(gain_one, "fsdp", axis=0, tiled=True),
        lax.all_gather(shift_one, "fsdp", axis=0, tiled=True),
        lax.all_gather(w_qkv, "fsdp", axis=1, tiled=True),
        lax.all_gather(w_attn_out, "fsdp", axis=1, tiled=True),
        lax.all_gather(gain_two, "fsdp", axis=0, tiled=True),
        lax.all_gather(shift_two, "fsdp", axis=0, tiled=True),
        lax.all_gather(w_router, "fsdp", axis=0, tiled=True),
        lax.all_gather(w_in, "fsdp", axis=1, tiled=True),
        lax.all_gather(w_out, "fsdp", axis=2, tiled=True),
    )
    own_rows = tokens.shape[0]
    width = tokens.shape[1]
    experts = w_in.shape[0]
    groups = lax.axis_size("tensor")
    capacity = groups * MOST
    gain_one_f = gain_one_all.astype(jnp.float32)
    shift_one_f = shift_one_all.astype(jnp.float32)
    gain_two_f = gain_two_all.astype(jnp.float32)
    shift_two_f = shift_two_all.astype(jnp.float32)
    resident = tokens.astype(jnp.float32)
    normed_one = layer_norm(resident, gain_one_f, shift_one_f).astype(jnp.bfloat16)
    gathered_one = lax.all_gather(normed_one, "heads", axis=0, tiled=True)
    rows_group = gathered_one.shape[0]
    local_width = qkv_full.shape[2]
    local_heads = local_width // HD
    images = rows_group // SEQ
    projected = jnp.einsum(
        "td,cdk->ctk", gathered_one, qkv_full, preferred_element_type=jnp.float32
    ).astype(jnp.bfloat16)
    pieces = projected.reshape(3, images, SEQ, local_heads, HD)
    scores = (
        jnp.einsum("ishd,ithd->ihst", pieces[0], pieces[1], preferred_element_type=jnp.float32)
        * 0.125
    )
    log_total = jax.nn.logsumexp(scores, axis=-1, keepdims=True)
    weights_att = jnp.exp(scores - log_total)
    weights_low = weights_att.astype(jnp.bfloat16)
    attn_mix = jnp.einsum(
        "ihst,ithd->ishd", weights_low, pieces[2], preferred_element_type=jnp.float32
    )
    attn_mix = attn_mix.astype(jnp.bfloat16).reshape(rows_group, local_width)
    attended = lax.psum_scatter(
        jnp.dot(attn_mix, attn_out_full, preferred_element_type=jnp.float32).astype(jnp.bfloat16),
        "heads",
        scatter_dimension=0,
        tiled=True,
    ).astype(jnp.float32)
    resid = resident + attended
    normed_two = layer_norm(resid, gain_two_f, shift_two_f).astype(jnp.bfloat16)
    gathered_two, cot_group = (
        lax.all_gather(normed_two, "tensor", axis=0, tiled=True),
        lax.all_gather(cotangent, "tensor", axis=0, tiled=True),
    )
    rows_two = gathered_two.shape[0]
    logits = jnp.dot(gathered_two, router_full, preferred_element_type=jnp.float32)
    router = jax.nn.softmax(logits, axis=-1)
    chosen = (routes[:, :, None] == jnp.arange(experts, dtype=jnp.int32)).astype(jnp.float32)
    gates = jnp.sum(router[:, None, :] * chosen, -1)
    per_block = chosen.reshape(groups, own_rows * 2, experts)
    earlier = jnp.cumsum(per_block, axis=1) - per_block
    position = jnp.sum(earlier * per_block, -1).astype(jnp.int32).reshape(rows_two * 2)
    source = jnp.arange(rows_two * 2, dtype=jnp.int32) // (own_rows * 2)
    expert_of = routes.reshape(rows_two * 2)
    slot_index = expert_of * capacity + source * MOST + position
    token_of = jnp.arange(rows_two * 2, dtype=jnp.int32) // 2
    dispatched = (
        jnp.zeros((experts * capacity, width), jnp.bfloat16)
        .at[slot_index]
        .set(gathered_two[token_of])
    )
    dispatched = dispatched.reshape(experts, capacity, width)
    inner = jnp.einsum("ecd,edf->ecf", dispatched, inner_full, preferred_element_type=jnp.float32)
    activated, gelu_back = jax.vjp(jax.nn.gelu, inner)
    hidden = activated.astype(jnp.bfloat16)
    partial_out = jnp.einsum("ecf,efd->ecd", hidden, outer_full, preferred_element_type=jnp.float32)
    picked = partial_out.reshape(experts * capacity, width)[slot_index].reshape(rows_two, 2, width)
    cot_float = cot_group.astype(jnp.float32)
    mixture = jnp.sum(gates[:, :, None] * picked, 1)
    gate_terms = jnp.sum(cot_float[:, None, :] * picked, -1)
    mixture_own, gate_grad = (
        lax.psum_scatter(
            mixture.astype(jnp.bfloat16), "tensor", scatter_dimension=0, tiled=True
        ).astype(jnp.float32),
        lax.psum_scatter(
            gate_terms.astype(jnp.bfloat16), "tensor", scatter_dimension=0, tiled=True
        ).astype(jnp.float32),
    )
    output = (resid + mixture_own).astype(jnp.bfloat16)
    slot_grads = (gates[:, :, None] * cot_float[:, None, :]).reshape(rows_two * 2, width)
    result_grad = jnp.zeros((experts * capacity, width), jnp.float32).at[slot_index].set(slot_grads)
    result_grad = result_grad.astype(jnp.bfloat16).reshape(experts, capacity, width)
    grad_outer = jnp.einsum("ecf,ecd->efd", hidden, result_grad, preferred_element_type=jnp.float32)
    hidden_grad = jnp.einsum(
        "ecd,efd->ecf", result_grad, outer_full, preferred_element_type=jnp.float32
    )
    inner_grad = gelu_back(hidden_grad)[0].astype(jnp.bfloat16)
    grad_inner = jnp.einsum(
        "ecd,ecf->edf", dispatched, inner_grad, preferred_element_type=jnp.float32
    )
    back_rows = jnp.einsum(
        "ecf,edf->ecd", inner_grad, inner_full, preferred_element_type=jnp.float32
    )
    token_grad = jnp.sum(
        back_rows.reshape(experts * capacity, width)[slot_index].reshape(rows_two, 2, width), 1
    )
    normed_two_grad = lax.psum_scatter(
        token_grad.astype(jnp.bfloat16), "tensor", scatter_dimension=0, tiled=True
    ).astype(jnp.float32)
    offset = lax.axis_index("tensor") * own_rows
    router_own = lax.dynamic_slice_in_dim(router, offset, own_rows, 0)
    chosen_own = lax.dynamic_slice_in_dim(chosen, offset, own_rows, 0)
    prob_grad = jnp.sum(gate_grad[:, :, None] * chosen_own, 1)
    logit_grad = router_own * (prob_grad - jnp.sum(router_own * prob_grad, -1, keepdims=True))
    logit_grad = logit_grad.astype(jnp.bfloat16)
    grad_router = jnp.einsum(
        "td,te->de", normed_two, logit_grad, preferred_element_type=jnp.float32
    )
    normed_two_grad = normed_two_grad + jnp.einsum(
        "te,de->td", logit_grad, router_full, preferred_element_type=jnp.float32
    )
    unused_two, norm_two_back = jax.vjp(layer_norm, resid, gain_two_f, shift_two_f)
    resid_back, grad_gain_two, grad_shift_two = norm_two_back(normed_two_grad)
    resid_grad = cotangent.astype(jnp.float32) + resid_back
    attn_grad_own = resid_grad.astype(jnp.bfloat16)
    attended_grad = lax.all_gather(attn_grad_own, "heads", axis=0, tiled=True)
    grad_attn_out = jnp.einsum(
        "tk,td->kd", attn_mix, attended_grad, preferred_element_type=jnp.float32
    )
    mix_grad = jnp.einsum(
        "td,kd->tk", attended_grad, attn_out_full, preferred_element_type=jnp.float32
    ).astype(jnp.bfloat16)
    mix_grad = mix_grad.reshape(images, SEQ, local_heads, HD)
    scores_again = (
        jnp.einsum("ishd,ithd->ihst", pieces[0], pieces[1], preferred_element_type=jnp.float32)
        * 0.125
    )
    weights_again = jnp.exp(scores_again - log_total)
    weight_grad = jnp.einsum(
        "ishd,ithd->ihst", mix_grad, pieces[2], preferred_element_type=jnp.float32
    )
    score_grad = weights_again * (
        weight_grad - jnp.sum(weights_again * weight_grad, -1, keepdims=True)
    )
    score_grad = score_grad.astype(jnp.bfloat16)
    query_grad = (
        jnp.einsum("ihst,ithd->ishd", score_grad, pieces[1], preferred_element_type=jnp.float32)
        * 0.125
    )
    key_grad = (
        jnp.einsum("ihst,ishd->ithd", score_grad, pieces[0], preferred_element_type=jnp.float32)
        * 0.125
    )
    value_grad = jnp.einsum(
        "ihst,ishd->ithd",
        weights_again.astype(jnp.bfloat16),
        mix_grad,
        preferred_element_type=jnp.float32,
    )
    qkv_back = (
        jnp.stack([query_grad, key_grad, value_grad])
        .astype(jnp.bfloat16)
        .reshape(3, rows_group, local_width)
    )
    grad_qkv = jnp.einsum("td,ctk->cdk", gathered_one, qkv_back, preferred_element_type=jnp.float32)
    normed_one_grad = lax.psum_scatter(
        jnp.einsum("ctk,cdk->td", qkv_back, qkv_full, preferred_element_type=jnp.float32).astype(
            jnp.bfloat16
        ),
        "heads",
        scatter_dimension=0,
        tiled=True,
    ).astype(jnp.float32)
    unused_one, norm_one_back = jax.vjp(layer_norm, resident, gain_one_f, shift_one_f)
    input_back, grad_gain_one, grad_shift_one = norm_one_back(normed_one_grad)
    input_grad = (resid_grad + input_back).astype(jnp.bfloat16)
    sum_gain_one, sum_shift_one, sum_gain_two, sum_shift_two, sum_router, sum_inner, sum_outer = (
        lax.psum_scatter(grad_gain_one, ("fsdp", "heads"), scatter_dimension=0, tiled=True),
        lax.psum_scatter(grad_shift_one, ("fsdp", "heads"), scatter_dimension=0, tiled=True),
        lax.psum_scatter(grad_gain_two, ("fsdp", "heads"), scatter_dimension=0, tiled=True),
        lax.psum_scatter(grad_shift_two, ("fsdp", "heads"), scatter_dimension=0, tiled=True),
        lax.psum_scatter(grad_router, ("fsdp", "heads"), scatter_dimension=0, tiled=True),
        lax.psum_scatter(grad_inner, ("fsdp", "heads"), scatter_dimension=1, tiled=True),
        lax.psum_scatter(grad_outer, ("fsdp", "heads"), scatter_dimension=2, tiled=True),
    )
    sum_gain_one, sum_shift_one, sum_gain_two, sum_shift_two, sum_router, sum_inner, sum_outer = (
        lax.all_gather(sum_gain_one.astype(jnp.bfloat16), "heads", axis=0, tiled=True).astype(
            sum_gain_one.dtype
        ),
        lax.all_gather(sum_shift_one.astype(jnp.bfloat16), "heads", axis=0, tiled=True).astype(
            sum_shift_one.dtype
        ),
        lax.all_gather(sum_gain_two.astype(jnp.bfloat16), "heads", axis=0, tiled=True).astype(
            sum_gain_two.dtype
        ),
        lax.all_gather(sum_shift_two.astype(jnp.bfloat16), "heads", axis=0, tiled=True).astype(
            sum_shift_two.dtype
        ),
        lax.all_gather(sum_router.astype(jnp.bfloat16), "heads", axis=0, tiled=True).astype(
            sum_router.dtype
        ),
        lax.all_gather(sum_inner.astype(jnp.bfloat16), "heads", axis=1, tiled=True).astype(
            sum_inner.dtype
        ),
        lax.all_gather(sum_outer.astype(jnp.bfloat16), "heads", axis=2, tiled=True).astype(
            sum_outer.dtype
        ),
    )
    sum_qkv, sum_attn_out = (
        lax.psum_scatter(
            grad_qkv.astype(jnp.bfloat16), "fsdp", scatter_dimension=1, tiled=True
        ).astype(jnp.float32),
        lax.psum_scatter(
            grad_attn_out.astype(jnp.bfloat16), "fsdp", scatter_dimension=1, tiled=True
        ).astype(jnp.float32),
    )
    sum_qkv, sum_attn_out, sum_gain_one, sum_shift_one, sum_gain_two, sum_shift_two, sum_router = (
        lax.psum(sum_qkv.astype(jnp.bfloat16), "tensor").astype(jnp.float32),
        lax.psum(sum_attn_out.astype(jnp.bfloat16), "tensor").astype(jnp.float32),
        lax.psum(sum_gain_one.astype(jnp.bfloat16), "tensor").astype(jnp.float32),
        lax.psum(sum_shift_one.astype(jnp.bfloat16), "tensor").astype(jnp.float32),
        lax.psum(sum_gain_two.astype(jnp.bfloat16), "tensor").astype(jnp.float32),
        lax.psum(sum_shift_two.astype(jnp.bfloat16), "tensor").astype(jnp.float32),
        lax.psum(sum_router.astype(jnp.bfloat16), "tensor").astype(jnp.float32),
    )
    return (
        output,
        input_grad,
        sum_gain_one,
        sum_shift_one,
        sum_qkv,
        sum_attn_out,
        sum_gain_two,
        sum_shift_two,
        sum_router,
        sum_inner,
        sum_outer,
    )


def solution(mesh):
    placed = (
        P(("fsdp", "heads", "tensor"), None),
        P("fsdp"),
        P("fsdp"),
        P(None, "fsdp", "heads"),
        P("heads", "fsdp"),
        P("fsdp"),
        P("fsdp"),
        P("fsdp", None),
        P(None, "fsdp", "tensor"),
        P(None, "tensor", "fsdp"),
        P(("fsdp", "heads"), None),
        P(("fsdp", "heads", "tensor"), None),
    )
    return jax.shard_map(
        local,
        mesh=mesh,
        in_specs=placed,
        out_specs=(
            P(("fsdp", "heads", "tensor"), None),
            P(("fsdp", "heads", "tensor"), None),
            P("fsdp"),
            P("fsdp"),
            P(None, "fsdp", "heads"),
            P("heads", "fsdp"),
            P("fsdp"),
            P("fsdp"),
            P("fsdp", None),
            P(None, "fsdp", "tensor"),
            P(None, "tensor", "fsdp"),
        ),
        check_vma=False,
    )
```

profile of v0, /device:TPU:0, one launch (start us, length us, event | category | flops | bytes accessed | tf_op | source)
XLA Modules:
  0.0 914.5 jit_solution(13877523563513534780)
XLA Ops:
  36.3 27.4 %all-gather.26.cloned.1.call-done = bf16[4,394,512]{2,1,0:T(8,128)(2,1)} async-done(((bf16[1,394,512]{2,1,0:T(8,128)(2,1)}), bf16[4,394,512]{2,1,0:T(8,128)(2,1)}) %all-gather.26.cloned.1.call-update) | async-done | bytes 1613840 | tf_op jit(solution)/shard_map/all_gather | solution.py:64
  85.6 35.1 %fusion = bf16[400,512]{1,0:T(8,128)(2,1)} fusion(bf16[1576,512]{1,0:T(8,128)(2,1)} %convolution_convert_fusion), kind=kCustom, calls=%all-reduce-scatter | all-reduce-scatter fusion | flops 819201 | bytes 2023936
  174.1 9.9 %mul.302 = f32[1576,2,512]{2,1,0:T(2,128)} broadcast(f32[1576,512]{1,0:T(8,128)} %reshape.376), dimensions={0,2} | broadcast | bytes 9682944 | tf_op jit(solution)/shard_map/mul | solution.py:131
  183.9 8.5 mul.303
  200.3 30.7 %scatter_custom_fusion.1 = f32[3936,512]{1,0:T(8,128)} fusion(s32[3152]{0:T(1024)S(1)} %fusion.52, f32[3152,512]{1,0:T(8,128)} %mul.303, f32[]{:T(128)} %constant.29.clone.1, f32[3152]{0:T(1024)S(1)} %mul.300), kind=kCustom, calls=%fused_computation.16 | custom fusion | flops 1613824 | bytes 14532612 | tf_op jit(solution)/shard_map/scatter | solution.py:132
  236.7 46.4 %scatter_custom_fusion = bf16[3936,512]{1,0:T(8,128)(2,1)} fusion(s32[3152]{0:T(1024)S(1)} %fusion.52, bf16[1576,512]{1,0:T(8,128)(2,1)} %reshape.365, s32[4096]{0:T(1024)} %pad_clamp_fusion.1, bf16[]{:T(256)} %constant.66.clone.1), kind=kCustom, calls=%fused_computation.25 | custom fusion | bytes 4030976 | tf_op jit(solution)/shard_map/scatter | solution.py:111
  291.4 12.5 %fusion.11 = (bf16[4,984,512]{2,1,0:T(8,128)(2,1)}, f32[4,984,512]{2,1,0:T(8,128)S(1)}) fusion(f32[4,984,512]{2,1,0:T(8,128)} %fusion.69, bf16[4,984,512]{2,1,0:T(8,128)(2,1)} %bitcast.99, bf16[4,512,512]{2,1,0:T(8,128)(2,1)} %all-gather.18.cloned.1.call-done), kind=kOutput, calls=%fused_computation.13 | convolution fusion | flops 2103902208 | bytes 26279936 | tf_op jit(solution)/shard_map/ecd,edf->ecf/dot_general | solution.py:114
  309.5 14.1 %gather_fusion = f32[3152,512]{1,0:T(8,128)} fusion(f32[3936,512]{1,0:T(8,128)} %bitcast.96, s32[4096]{0:T(1024)S(1)} %pad_clamp_fusion), kind=kCustom, calls=%fused_computation.1 | custom fusion | bytes 12923200 | tf_op jit(solution)/shard_map/gather | solution.py:118
  323.6 8.3 reshape.296
  331.9 21.1 %multiply_reduce_fusion = (bf16[1576,2]{1,0:T(8,128)(2,1)}, bf16[1576,512]{1,0:T(8,128)(2,1)}) fusion(f32[1576,2,512]{2,1,0:T(2,128)} %reshape.296, f32[1576,512]{1,0:T(8,128)} %reshape.376, f32[1576,2]{1,0:T(8,128)} %copy.138), kind=kLoop, calls=%fused_computation.15 | loop fusion | flops 5645232 | bytes 11315680 | tf_op jit(solution)/shard_map/reduce_sum | solution.py:121
  358.5 14.1 %gather_fusion.1 = f32[3152,512]{1,0:T(8,128)} fusion(f32[3936,512]{1,0:T(8,128)} %bitcast.95, s32[4096]{0:T(1024)S(1)} %pad_clamp_fusion), kind=kCustom, calls=%fused_computation.2 | custom fusion | bytes 12923200 | tf_op jit(solution)/shard_map/gather | solution.py:146
  372.6 8.5 reshape.299
  381.0 27.8 %reduce_sum.209 = bf16[1576,512]{1,0:T(8,128)(2,1)} reduce(f32[1576,2,512]{2,1,0:T(2,128)} %reshape.299, f32[]{:T(128)} %constant.29.clone.1), dimensions={1}, to_apply=%region_17.18 | reduce | flops 806912 | bytes 8069124 | tf_op jit(solution)/shard_map/reduce_sum | solution.py:145
  408.8 36.3 %fusion.64 = (bf16[400,512]{1,0:T(8,128)(2,1)}, bf16[400,2]{1,0:T(8,128)(2,1)S(1)}, bf16[400,512]{1,0:T(8,128)(2,1)}) fusion(bf16[1576,512]{1,0:T(8,128)(2,1)} %get-tuple-element.67, bf16[1576,2]{1,0:T(8,128)(2,1)} %get-tuple-element.66, bf16[1576,512]{1,0:T(8,128)(2,1)} %reduce_sum.209), kind=kCustom, calls=%all-reduce-scatter.5 | all-reduce-scatter fusion | flops 1641601 | bytes 4055264
  478.5 35.4 %all-gather.32.cloned.1.call-done = bf16[4,394,512]{2,1,0:T(8,128)(2,1)} async-done(((bf16[1,394,512]{2,1,0:T(8,128)(2,1)}), bf16[4,394,512]{2,1,0:T(8,128)(2,1)}) %all-gather.32.cloned.1.call-update) | async-done | bytes 1613840 | tf_op jit(solution)/shard_map/all_gather | solution.py:167
  548.8 9.8 %fusion.62 = f32[4,512,512]{1,2,0:T(8,128)} fusion(bf16[4,984,512]{2,1,0:T(8,128)(2,1)} %bitcast.98, f32[4,984,512]{2,1,0:T(8,128)} %copy-done.37), kind=kOutput, calls=%fused_computation.138 | convolution fusion | flops 2081734656 | bytes 16285696 | tf_op jit(solution)/shard_map/ecf,ecd->efd/dot_general | solution.py:134
  569.4 83.5 %reduce-scatter.24.cloned.1.call-done = f32[4,512,64]{1,2,0:T(8,128)} async-done(((f32[4,512,512]{1,2,0:T(8,128)}), f32[4,512,64]{1,2,0:T(8,128)}) %reduce-scatter.24.cloned.1.call-update) | async-done | bytes 524304 | tf_op jit(solution)/shard_map/reduce_scatter | solution.py:225
  656.9 87.2 %reduce-scatter.22.cloned.1.call-done = f32[4,64,512]{2,1,0:T(8,128)} async-done(((f32[4,512,512]{2,1,0:T(8,128)}), f32[4,64,512]{2,1,0:T(8,128)}) %reduce-scatter.22.cloned.1.call-update) | async-done | bytes 524304 | tf_op jit(solution)/shard_map/reduce_scatter | solution.py:224
  745.9 37.3 %fusion.4 = bf16[400,512]{1,0:T(8,128)(2,1)} fusion(bf16[1576,512]{1,0:T(8,128)(2,1)S(1)} %fusion.18), kind=kCustom, calls=%all-reduce-scatter.4 | all-reduce-scatter fusion | flops 819201 | bytes 2023936
  787.6 24.4 %reduce-scatter.26.cloned.1.call-done = f32[64,4]{1,0:T(8,128)} async-done(((f32[512,4]{1,0:T(8,128)}), f32[64,4]{1,0:T(8,128)}) %reduce-scatter.26.cloned.1.call-update) | async-done | bytes 1040
  812.9 9.9 %all-gather.8 = bf16[4,64,4]{1,2,0:T(4,128)(2,1)S(1)} all-gather(bf16[1,64,4]{1,2,0:T(4,128)(2,1)S(1)} %bitcast.114), channel_id=1, replica_groups=mesh['fsdp'=2,'heads'=4,'tensor'=4] {'heads'}, dimensions={0}, use_global_device_ids=true | all-gather | bytes 2560 | tf_op jit(solution)/shard_map/all_gather | solution.py:240
  826.3 18.1 %all-reduce.19 = (bf16[512]{0:T(512)(128)(2,1)S(1)}, bf16[512]{0:T(512)(128)(2,1)S(1)}, bf16[512]{0:T(512)(128)(2,1)S(1)}, bf16[512]{0:T(512)(128)(2,1)S(1)}) all-reduce(f32[512]{0:T(512)S(1)} %get-tuple-element.71, f32[512]{0:T(512)S(1)} %get-tuple-element.73, ...), channel_id=7, replica_groups=mesh['fsdp'=2,'heads'=4,'tensor'=4] {'fsdp','heads'}, use_global_device_ids=true, to_apply=%region_30.31.clone | all-reduce | flops 2048 | bytes 12288
  845.6 9.7 %all-reduce.22 = (bf16[256]{0:T(256)(128)(2,1)S(1)}, bf16[256]{0:T(256)(128)(2,1)S(1)}, bf16[256]{0:T(256)(128)(2,1)S(1)}, bf16[256]{0:T(256)(128)(2,1)S(1)}) all-reduce(bf16[256]{0:T(256)(128)(2,1)S(1)} %dynamic-update-slice, bf16[256]{0:T(256)(128)(2,1)S(1)} %dynamic-update-slice.1, ...), channel_id=1, replica_groups=mesh['fsdp'=2,'heads'=4,'tensor'=4] {'heads'}, use_global_device_ids=true, to_apply=%add.1 | all-reduce | flops 1024 | bytes 4096
  878.4 26.3 %all-gather.22.cloned.1.call-done = bf16[4,256,512]{2,1,0:T(8,128)(2,1)} async-done(((bf16[4,64,512]{2,1,0:T(8,128)(2,1)}), bf16[4,256,512]{2,1,0:T(8,128)(2,1)}) %all-gather.22.cloned.1.call-update) | async-done | bytes 1048592 | tf_op jit(solution)/shard_map/all_gather | solution.py:243
  (277 shorter events, 254.6 us)
Async XLA Ops:
  7.2 56.5 %all-gather.26.cloned.1.call-start = ((), (), s32[]{:S(2)}) async-start(), calls=%async_computation.13 | async-start | bytes 2048000 | tf_op jit(solution)/shard_map/all_gather | solution.py:64
  23.5 147.0 %all-gather.30.cloned.1.call-start = ((), (), s32[]{:S(2)}) async-start(), calls=%async_computation.15 | async-start | bytes 2048000 | tf_op jit(solution)/shard_map/all_gather | solution.py:94
  24.2 168.2 %all-gather.28.cloned.1.call-start = ((), (), s32[]{:S(2)}) async-start(), calls=%async_computation.14 | async-start | bytes 2048000 | tf_op jit(solution)/shard_map/all_gather | solution.py:93
  121.5 11.7 %collective-permute-start = (bf16[18,512]{1,0:T(8,128)(2,1)S(1)}, bf16[18,512]{1,0:T(8,128)(2,1)S(1)}, u32[]{:S(2)}, u32[]{:S(2)}) collective-permute-start(bf16[18,512]{1,0:T(8,128)(2,1)S(1)} %slice.44), channel_id=1, source_target_pairs={{0,4},{4,8},{8,12},{1,5},{5,9},{9,13},{2,6},{6,10},{10,14},{3,7},{... | collective-permute-start | bytes 55304
  142.1 141.1 %all-gather.20.cloned.1.call-start = ((), (), s32[]{:S(2)}) async-start(), calls=%async_computation.6 | async-start | bytes 3145728 | tf_op jit(solution)/shard_map/all_gather | solution.py:51
  142.7 148.7 %all-gather.18.cloned.1.call-start = ((), (), s32[]{:S(2)}) async-start(), calls=%async_computation.5 | async-start | bytes 3145728 | tf_op jit(solution)/shard_map/all_gather | solution.py:50
  143.3 370.6 %all-gather.32.cloned.1.call-start = ((), (), s32[]{:S(2)}) async-start(), calls=%async_computation.16 | async-start | bytes 2048000 | tf_op jit(solution)/shard_map/all_gather | solution.py:167
  445.1 9.8 %collective-permute-start.3 = (bf16[18,2]{1,0:T(8,128)(2,1)S(1)}, bf16[18,2]{1,0:T(8,128)(2,1)}, u32[]{:S(2)}, u32[]{:S(2)}) collective-permute-start(bf16[18,2]{1,0:T(8,128)(2,1)S(1)} %slice.47), channel_id=1, source_target_pairs={{0,1},{1,2},{2,3},{4,5},{5,6},{6,7},{8,9},{9,10},{10,11},{12,13},{... | collective-permute-start | bytes 224
  449.6 11.2 %collective-permute-start.2 = (bf16[18,512]{1,0:T(8,128)(2,1)}, bf16[18,512]{1,0:T(8,128)(2,1)}, u32[]{:S(2)}, u32[]{:S(2)}) collective-permute-start(bf16[18,512]{1,0:T(8,128)(2,1)} %slice.46), channel_id=1, source_target_pairs={{0,1},{1,2},{2,3},{4,5},{5,6},{6,7},{8,9},{9,10},{10,11},{12,13},{... | collective-permute-start | bytes 55304
  452.9 16.0 %collective-permute-start.1 = (bf16[18,512]{1,0:T(8,128)(2,1)}, bf16[18,512]{1,0:T(8,128)(2,1)}, u32[]{:S(2)}, u32[]{:S(2)}) collective-permute-start(bf16[18,512]{1,0:T(8,128)(2,1)} %slice.45), channel_id=1, source_target_pairs={{0,1},{1,2},{2,3},{4,5},{5,6},{6,7},{8,9},{9,10},{10,11},{12,13},{... | collective-permute-start | bytes 55304
  478.4 90.5 %reduce-scatter.20.cloned.1.call-start = ((), (), s32[]{:S(2)}) async-start(), calls=%async_computation.8 | async-start | bytes 196608 | tf_op jit(solution)/shard_map/reduce_scatter | solution.py:254
  534.9 34.0 %reduce-scatter.18.cloned.1.call-start = ((), (), s32[]{:S(2)}) async-start(), calls=%async_computation.7 | async-start | bytes 589824 | tf_op jit(solution)/shard_map/reduce_scatter | solution.py:251
  548.8 104.2 %reduce-scatter.24.cloned.1.call-start = ((), (), s32[]{:S(2)}) async-start(), calls=%async_computation.11 | async-start | bytes 4718592 | tf_op jit(solution)/shard_map/reduce_scatter | solution.py:225
  558.7 185.4 %reduce-scatter.22.cloned.1.call-start = ((), (), s32[]{:S(2)}) async-start(), calls=%async_computation.9 | async-start | bytes 4718592 | tf_op jit(solution)/shard_map/reduce_scatter | solution.py:224
  566.7 245.3 %reduce-scatter.26.cloned.1.call-start = ((), (), s32[]{:S(2)}) async-start(), calls=%async_computation.17 | async-start | bytes 294912
  568.8 297.6 %all-reduce.26.cloned.1.call-start = ((), (), s32[]{:S(2)}) async-start(), calls=%async_computation.18 | async-start | bytes 524288 | tf_op jit(solution)/shard_map/psum | solution.py:259
  569.4 306.4 %all-gather.24.cloned.1.call-start = ((), (), s32[]{:S(2)}) async-start(), calls=%async_computation.12 | async-start | bytes 1310720 | tf_op jit(solution)/shard_map/all_gather | solution.py:246
  654.7 170.5 %copy-start = (bf16[394,512]{1,0:T(8,128)(2,1)S(1)}, bf16[394,512]{1,0:T(8,128)(2,1)}, u32[]{:S(2)}) copy-start(bf16[394,512]{1,0:T(8,128)(2,1)} %param.12) | copy-start | bytes 1210372
  654.8 170.5 %copy-start.19 = (f32[394]{0:T(512)S(1)}, f32[394]{0:T(512)}, u32[]{:S(2)}) copy-start(f32[394]{0:T(512)} %copy-done.18) | copy-start | bytes 4732
  654.8 170.5 %copy-start.21 = (f32[2,1,256]{2,1,0:T(1,128)S(1)}, f32[2,1,256]{2,1,0:T(1,128)}, u32[]{:S(2)}) copy-start(f32[2,1,256]{2,1,0:T(1,128)} %copy-done.20) | copy-start | bytes 6148
  654.8 170.9 %copy-start.28 = (f32[394]{0:T(512)S(1)}, f32[394]{0:T(512)}, u32[]{:S(2)}) copy-start(f32[394]{0:T(512)} %copy-done.27) | copy-start | bytes 4732
  654.8 249.9 %all-gather.22.cloned.1.call-start = ((), (), s32[]{:S(2)}) async-start(), calls=%async_computation.10 | async-start | bytes 1310720 | tf_op jit(solution)/shard_map/all_gather | solution.py:243
  656.9 207.3 %copy-start.3 = (f32[394,512]{1,0:T(8,128)S(1)}, f32[394,512]{1,0:T(8,128)}, u32[]{:S(2)}) copy-start(f32[394,512]{1,0:T(8,128)} %copy-done.2) | copy-start | bytes 2420740
  783.9 39.0 %collective-permute-start.4 = (bf16[18,512]{1,0:T(8,128)(2,1)S(1)}, bf16[18,512]{1,0:T(8,128)(2,1)S(1)}, u32[]{:S(2)}, u32[]{:S(2)}) collective-permute-start(bf16[18,512]{1,0:T(8,128)(2,1)S(1)} %slice.48), channel_id=1, source_target_pairs={{0,4},{4,8},{8,12},{1,5},{5,9},{9,13},{2,6},{6,10},{10,14},{3,7},{... | collective-permute-start | bytes 55304
  (33 other events, 712.4 us)
Sparse Core Ops, SparseCore 0:
  23.6 39.9 all-gather.25
  65.2 18.8 all-gather.29
  142.2 18.0 all-gather.27
  161.7 33.0 all-gather.19
  196.2 33.1 all-gather.17
  478.5 35.3 all-gather.31
  535.0 9.0 reduce-scatter.19
  548.9 11.9 reduce-scatter.17
  565.0 87.9 reduce-scatter.23
  656.4 87.6 reduce-scatter.21
  747.8 64.2 reduce-scatter.25
  814.4 31.1 all-reduce.25
  847.8 27.9 all-gather.23
  877.2 27.4 all-gather.21
where the time goes:
time: 927 us; the launch traced here: 914 us
  waiting for transfers between devices  293 us (32%)
  local copies, waits for them, and re-layouts  199 us (21%)
  blocking collectives  187 us (20%)
  other arithmetic  130 us (14%)
  matrix products  76.1 us (8%)
  between operations  17.7 us (2%)
  starting transfers between devices  11.5 us (1%)
    unnamed x5, blocking collectives  136 us
    reduce_scatter x1, waiting for transfers between devices, local(): lax.psum_scatter(grad_inner, ('fsdp', 'heads'), scatter_dimension=1, tile...  87.2 us
    reduce_scatter x1, waiting for transfers between devices, local(): lax.psum_scatter(grad_outer, ('fsdp', 'heads'), scatter_dimension=2, tile...  83.5 us
    unnamed x116, local copies, waits for them, and re-layouts  46.6 us
    scatter x1, local copies, waits for them, and re-layouts, local(): dispatched = jnp.zeros((experts * capacity, width), jnp.bfloat16).at[slot...  46.4 us
    all_gather x1, waiting for transfers between devices, local(): attended_grad = lax.all_gather(attn_grad_own, 'heads', axis=0, tiled=True)  35.4 us
    scatter x1, other arithmetic, local(): jnp.zeros((experts * capacity, width), jnp.float32).at[slot_index]  30.7 us
    reduce_sum x1, other arithmetic, local(): jnp.sum(back_rows.reshape(experts * capacity, width)[slot_index].reshape(...  27.8 us
  transfers between devices with their start and end apart: 19, of which 7 were waited for; matrix products, arithmetic and copies ran while one was open for 35% of the time, Pallas kernels for 0%

commit v1 on v0

v1 whole, which is shorter than its diff:
```python
import functools

import jax
import jax.numpy as jnp
from jax import lax
from jax.experimental import pallas as pl
from jax.experimental.pallas import tpu as pltpu
from jax.sharding import PartitionSpec as P

HD = 64
SEQ = 197
PAD = 208
ROWS = 2 * PAD
D = 512
FFT = 512
EXPERTS = 4
BF = jnp.bfloat16
F32 = jnp.float32
VMEM_LIMIT = 56 * 1024 * 1024
GELU_C = 0.7978845608028654


def nn(a, b):
    return lax.dot_general(a, b, (((1,), (0,)), ((), ())), preferred_element_type=F32)


def nt(a, b):
    return lax.dot_general(a, b, (((1,), (1,)), ((), ())), preferred_element_type=F32)


def tn(a, b):
    return lax.dot_general(a, b, (((0,), (0,)), ((), ())), preferred_element_type=F32)


def params(sem=None):
    return pltpu.CompilerParams(vmem_limit_bytes=VMEM_LIMIT, dimension_semantics=sem)


def smem():
    return pl.BlockSpec(memory_space=pltpu.SMEM)


def vmem():
    return pl.BlockSpec(memory_space=pltpu.VMEM)


def sds(shape, dtype):
    return jax.ShapeDtypeStruct(shape, dtype)


def call(kernel, outs, args, scratch=()):
    return pl.pallas_call(
        kernel,
        out_shape=outs,
        in_specs=[smem()] + [vmem()] * (len(args) - 1),
        out_specs=[vmem()] * len(outs),
        scratch_shapes=list(scratch),
        compiler_params=params(),
    )(*args)


def pack_kernel(idx, wqkv, wo, out):
    c = idx[1]
    rows = pl.ds(pl.multiple_of(c * 128, 128), 128)
    for i in range(3):
        out[i * 128 : (i + 1) * 128, :] = wqkv[i, rows, :]
    head = pl.ds(pl.multiple_of(c * 64, 64), 64)
    out[384:448, :] = wo[head, 0:128]
    out[448:512, :] = wo[head, 128:256]


def spread(v):
    zero = jnp.zeros((PAD - SEQ, v.shape[1]), v.dtype)
    return jnp.concatenate([v[:SEQ], zero, v[SEQ:], zero], axis=0)


def close(v):
    return jnp.concatenate([v[:SEQ], v[PAD : PAD + SEQ]], axis=0)


def pad_kernel(idx, tok, cot, tok_out, cot_out):
    tok_out[...] = spread(tok[...].astype(F32)).astype(BF)
    cot_out[...] = spread(cot[...].astype(F32)).astype(BF)


def norm_parts(x):
    center = jnp.mean(x, -1, keepdims=True)
    centered = x - center
    rstd = lax.rsqrt(jnp.mean(centered * centered, -1, keepdims=True) + 1e-06)
    return centered * rstd, rstd


def norm_back(xhat, rstd, grad, gain):
    dxhat = grad * gain
    m1 = jnp.mean(dxhat, -1, keepdims=True)
    m2 = jnp.mean(dxhat * xhat, -1, keepdims=True)
    return rstd * (dxhat - m1 - xhat * m2)


def attn_fwd_kernel(idx, tok, small, *refs):
    packs, (n1_ref, n2_ref, resid_ref, qkv_ref, mix_ref, wq_ref, wo_ref) = refs[:8], refs[8:]
    f, c = idx[0], idx[1]
    x = tok[...].astype(F32)
    xhat, _ = norm_parts(x)
    n1 = (xhat * small[4:5, :].astype(F32) + small[5:6, :].astype(F32)).astype(BF)
    n1_ref[...] = n1
    lane = lax.broadcasted_iota(jnp.int32, (PAD, 128), 1)
    key = lax.broadcasted_iota(jnp.int32, (PAD, PAD), 1)
    acc = [x[0:PAD], x[PAD:ROWS]]
    for j in range(4):
        for fr in range(2):
            fa = jnp.bitwise_xor(f, fr)
            for cr in range(2):
                ca = jnp.bitwise_xor(c, cr)
                src = packs[2 * j + cr]
                rows = pl.ds(pl.multiple_of(fa * 256 + ca * 128, 128), 128)
                for i in range(3):
                    wq_ref[j, rows, i * 128 : (i + 1) * 128] = src[fr, i * 128 : (i + 1) * 128, :]
                head = pl.ds(pl.multiple_of(ca * 64, 64), 64)
                for i in range(2):
                    cols = pl.ds(pl.multiple_of(fa * 256 + i * 128, 128), 128)
                    wo_ref[j, head, cols] = src[fr, 384 + 64 * i : 448 + 64 * i, :]
        qkv_ref[j] = nn(n1, wq_ref[j]).astype(BF)
        for im in range(2):
            r = slice(im * PAD, (im + 1) * PAD)
            q, k, v = (qkv_ref[j, r, i * 128 : (i + 1) * 128] for i in range(3))
            outs = []
            for head in range(2):
                s = nt(jnp.where(lane // HD == head, q, jnp.zeros_like(q)), k) * 0.125
                s = jnp.where(key < SEQ, s, -1e30)
                e = jnp.exp(s - jnp.max(s, -1, keepdims=True))
                p = e / jnp.sum(e, -1, keepdims=True)
                outs.append(nn(p.astype(BF), v))
            mix = jnp.where(lane < HD, outs[0], outs[1]).astype(BF)
            mix_ref[j, r, :] = mix
            acc[im] = acc[im] + nn(mix, wo_ref[j])
    for im in range(2):
        r = slice(im * PAD, (im + 1) * PAD)
        resid_ref[r, :] = acc[im]
        xhat, _ = norm_parts(acc[im])
        n2_ref[r, :] = (xhat * small[6:7, :].astype(F32) + small[7:8, :].astype(F32)).astype(BF)


def attn_bwd_kernel(idx, d0, d1, d2, resid, cot, tok, small, n1, qkv, mix, wq, wo, wrg, *refs):
    packs, (igrad, sgrad, dqkv_s, gq_s, go_s, dn1_s) = refs[:8], refs[8:]
    f, c = idx[0], idx[1]
    dn2 = d0[...].astype(F32) + d1[...].astype(F32) + d2[...].astype(F32)
    xhat, rstd = norm_parts(resid[...])
    sgrad[0:4, :] = wrg[0:4, :]
    sgrad[6:7, :] = jnp.sum(dn2 * xhat, 0, keepdims=True)
    sgrad[7:8, :] = jnp.sum(dn2, 0, keepdims=True)
    dresid = cot[...].astype(F32) + norm_back(xhat, rstd, dn2, small[6:7, :].astype(F32))
    resid_grad = dresid
    dattn = dresid.astype(BF)
    lane = lax.broadcasted_iota(jnp.int32, (PAD, 128), 1)
    key = lax.broadcasted_iota(jnp.int32, (PAD, PAD), 0)
    n1t = n1[...].T
    for j in range(4):
        go_s[...] = tn(mix[j], dattn).astype(BF)
        dmix = nt(dattn, wo[j]).astype(BF)
        for im in range(2):
            r = slice(im * PAD, (im + 1) * PAD)
            q, k, v = (qkv[j, r, i * 128 : (i + 1) * 128] for i in range(3))
            dm = dmix[r]
            dq, dk, dv = [], [], []
            for head in range(2):
                keep = lane // HD == head
                s = nt(k, jnp.where(keep, q, jnp.zeros_like(q))) * 0.125
                s = jnp.where(key < SEQ, s, -1e30)
                e = jnp.exp(s - jnp.max(s, 0, keepdims=True))
                p = e / jnp.sum(e, 0, keepdims=True)
                dp = nt(v, jnp.where(keep, dm, jnp.zeros_like(dm)))
                ds = (p * (dp - jnp.sum(p * dp, 0, keepdims=True))).astype(BF)
                dq.append(tn(ds, k))
                dk.append(nn(ds, q))
                dv.append(nn(p.astype(BF), dm))
            first = lane < HD
            dqkv_s[r, 0:128] = (jnp.where(first, dq[0], dq[1]) * 0.125).astype(BF)
            dqkv_s[r, 128:256] = (jnp.where(first, dk[0], dk[1]) * 0.125).astype(BF)
            dqkv_s[r, 256:384] = jnp.where(first, dv[0], dv[1]).astype(BF)
        dqkv = dqkv_s[...]
        gq_s[...] = nn(n1t, dqkv).astype(BF)
        part = nt(dqkv, wq[j])
        if j == 0:
            dn1_s[...] = part
        else:
            dn1_s[...] += part
        for fr in range(2):
            fa = jnp.bitwise_xor(f, fr)
            for cr in range(2):
                ca = jnp.bitwise_xor(c, cr)
                dst = packs[2 * j + cr]
                rows = pl.ds(pl.multiple_of(fa * 256 + ca * 128, 128), 128)
                for i in range(3):
                    dst[fr, i * 128 : (i + 1) * 128, :] = gq_s[rows, i * 128 : (i + 1) * 128]
                head = pl.ds(pl.multiple_of(ca * 64, 64), 64)
                for i in range(2):
                    cols = pl.ds(pl.multiple_of(fa * 256 + i * 128, 128), 128)
                    dst[fr, 384 + 64 * i : 448 + 64 * i, :] = go_s[head, cols]
    dn1 = dn1_s[...]
    xhat, rstd = norm_parts(tok[...].astype(F32))
    sgrad[4:5, :] = jnp.sum(dn1 * xhat, 0, keepdims=True)
    sgrad[5:6, :] = jnp.sum(dn1, 0, keepdims=True)
    grad = resid_grad + norm_back(xhat, rstd, dn1, small[4:5, :].astype(F32))
    igrad[...] = close(grad).astype(BF)


def out_kernel(idx, resid, m0, m1, m2, out):
    total = resid[...] + m0[...].astype(F32) + m1[...].astype(F32) + m2[...].astype(F32)
    out[...] = close(total).astype(BF)


def moe_kernel(final, idx, x0, x1, g0, g1, sel, small, win_a, win_b, wout_a, wout_b, *refs):
    if final:
        gin_in, gout_in, refs = refs[0], refs[1], refs[2:]
        keep, send, refs = refs[0], refs[1], refs[2:]
    else:
        gin_out, gout_out, refs = refs[0], refs[1], refs[2:]
    mix0, mix1, dn0, dn1, wrg, win, wout, xt, gt, gates, router, dprob, mix_s, dn_s, gin_s, gout_s = refs
    e = pl.program_id(0)
    f, t = idx[0], idx[2]
    xs, gs = (x0, x1), (g0, g1)
    base = 2 if final else 0
    lane = lax.broadcasted_iota(jnp.int32, (ROWS, 8), 1)

    @pl.when(e == 0)
    def _():
        dprob[...] = jnp.zeros_like(dprob)
        mix_s[...] = jnp.zeros_like(mix_s)
        dn_s[...] = jnp.zeros_like(dn_s)
        for b in range(2):
            xt[b] = xs[b][...].T
            gt[b] = gs[b][...].T
            logits = nt(xs[b][...], small[...])
            logits = jnp.where(lane < EXPERTS, logits, -1e30)
            ex = jnp.exp(logits - jnp.max(logits, -1, keepdims=True))
            prob = ex / jnp.sum(ex, -1, keepdims=True)
            router[b] = prob
            gates[b] = prob * sel[jnp.bitwise_xor(t, base + b)]

    own = pl.ds(pl.multiple_of(f * 256, 256), 256)
    oth = pl.ds(pl.multiple_of((1 - f) * 256, 256), 256)
    win[own, :] = win_a[0]
    win[oth, :] = win_b[0]
    wout[:, own] = wout_a[0]
    wout[:, oth] = wout_b[0]
    gin = gout = None
    for b in range(2):
        inner = nn(xs[b][...], win[...])
        back = nt(gs[b][...], wout[...])
        gate = jnp.sum(jnp.where(lane == e, gates[b], 0.0), -1, keepdims=True)
        square = inner * inner
        th = jnp.tanh(GELU_C * inner * (1.0 + 0.044715 * square))
        half = 0.5 * (1.0 + th)
        hidden = inner * half
        slope = half + 0.5 * inner * (1.0 - th * th) * (GELU_C * (1.0 + (3 * 0.044715) * square))
        dprob[b] += jnp.where(lane == e, jnp.sum(hidden * back, -1, keepdims=True), 0.0)
        hg = (gate * hidden).astype(BF)
        di = (gate * back * slope).astype(BF)
        mix_s[b] += nn(hg, wout[...])
        dn_s[b] += nt(di, win[...])
        part_in, part_out = nn(xt[b], di), nn(gt[b], hg)
        gin = part_in if gin is None else gin + part_in
        gout = part_out if gout is None else gout + part_out
    if final:
        gin_s[...] = (gin + gin_in[0]).astype(BF)
        gout_s[...] = (gout + gout_in[0]).astype(BF)
        for dst, rows in ((keep, own), (send, oth)):
            dst[0, 0:256, :] = gin_s[rows, :]
            dst[0, 256:512, :] = gout_s[rows, :]
    else:
        gin_out[0] = gin
        gout_out[0] = gout

    @pl.when(e == pl.num_programs(0) - 1)
    def _():
        for b, dn, mx in ((0, dn0, mix0), (1, dn1, mix1)):
            chosen = sel[jnp.bitwise_xor(t, base + b)]
            dp = dprob[b] * chosen
            dl = router[b] * (dp - jnp.sum(router[b] * dp, -1, keepdims=True))
            dl = jnp.where(lane < EXPERTS, dl, 0.0).astype(BF)
            dn[...] = (dn_s[b] + nn(dl, small[...])).astype(BF)
            mx[...] = mix_s[b].astype(BF)
            part = tn(dl, xs[b][...])
            if b == 0:
                wrg[...] = part
            else:
                wrg[...] += part


def moe(final, idx, xs, gs, sel, small, weights, carried):
    whole = lambda shape: pl.BlockSpec(shape, lambda e: (0,) * len(shape))
    expert = lambda shape: pl.BlockSpec((1,) + shape, lambda e: (e, 0, 0))
    row = whole((ROWS, D))
    in_specs = [smem(), row, row, row, row, whole((4, ROWS, 8)), whole((8, D))]
    in_specs += [expert((256, FFT))] * 2 + [expert((FFT, 256))] * 2
    outs, out_specs = [], []
    if final:
        in_specs += [expert((D, FFT))] * 2
        outs += [sds((EXPERTS, D, FFT), BF)] * 2
    else:
        outs += [sds((EXPERTS, D, FFT), F32)] * 2
    out_specs += [expert((D, FFT))] * 2
    outs += [sds((ROWS, D), BF)] * 4 + [sds((8, D), F32)]
    out_specs += [row] * 4 + [whole((8, D))]
    scratch = [
        pltpu.VMEM((D, FFT), BF),
        pltpu.VMEM((FFT, D), BF),
        pltpu.VMEM((2, D, ROWS), BF),
        pltpu.VMEM((2, D, ROWS), BF),
        pltpu.VMEM((2, ROWS, 8), F32),
        pltpu.VMEM((2, ROWS, 8), F32),
        pltpu.VMEM((2, ROWS, 8), F32),
        pltpu.VMEM((2, ROWS, D), F32),
        pltpu.VMEM((2, ROWS, D), F32),
        pltpu.VMEM((D, FFT), BF),
        pltpu.VMEM((D, FFT), BF),
    ]
    return pl.pallas_call(
        functools.partial(moe_kernel, final),
        grid=(EXPERTS,),
        out_shape=outs,
        in_specs=in_specs,
        out_specs=out_specs,
        scratch_shapes=scratch,
        compiler_params=params(("arbitrary",)),
    )(idx, *xs, *gs, sel, small, *weights, *carried)


def finish_kernel(idx, total, win_grad, wout_grad):
    win_grad[0] = total[0, 0:256, :].astype(F32)
    wout_grad[0] = total[0, 256:512, :].astype(F32).T


def finish(idx, total):
    expert = lambda shape: pl.BlockSpec((1,) + shape, lambda e: (e, 0, 0))
    return pl.pallas_call(
        finish_kernel,
        grid=(EXPERTS,),
        out_shape=[sds((EXPERTS, 256, FFT), F32), sds((EXPERTS, FFT, 256), F32)],
        in_specs=[smem(), expert((512, FFT))],
        out_specs=[expert((256, FFT)), expert((FFT, 256))],
        compiler_params=params(("arbitrary",)),
    )(idx, total)


def unpack_kernel(idx, own, sib, qkv_grad, o_grad):
    c = idx[1]
    for src, ca in ((own, c), (sib, 1 - c)):
        rows = pl.ds(pl.multiple_of(ca * 128, 128), 128)
        for i in range(3):
            qkv_grad[i, rows, :] = src[i * 128 : (i + 1) * 128, :].astype(F32)
        head = pl.ds(pl.multiple_of(ca * 64, 64), 64)
        o_grad[head, 0:128] = src[384:448, :].astype(F32)
        o_grad[head, 128:256] = src[448:512, :].astype(F32)


def flip(x, axis, bit):
    n = lax.axis_size(axis)
    return lax.ppermute(x, axis, [(i, i ^ bit) for i in range(n)])


def core(x):
    return flip(x, "tensor", 1)


def across(x):
    return flip(x, "tensor", 2)


def other(x):
    return flip(x, "fsdp", 1)


def plus(*parts):
    return functools.reduce(jnp.add, [p.astype(F32) for p in parts])


def packs_of_whole(qkv, out):
    packs = []
    for j in range(4):
        for cr in range(2):
            pair = []
            for fr in range(2):
                at = fr * 256 + cr * 128
                head = out[j * 128 + cr * 64 : j * 128 + cr * 64 + 64, fr * 256 : fr * 256 + 256]
                pair.append(
                    jnp.concatenate(
                        [qkv[i, at : at + 128, j * 128 : (j + 1) * 128] for i in range(3)]
                        + [head[:, :128], head[:, 128:]]
                    )
                )
            packs.append(jnp.stack(pair))
    return packs


def whole_of_packs(packs):
    qkv, out = jnp.zeros((3, D, D), F32), jnp.zeros((D, D), F32)
    for j in range(4):
        for cr in range(2):
            for fr in range(2):
                pack = packs[2 * j + cr][fr].astype(F32)
                at, hd = fr * 256 + cr * 128, j * 128 + cr * 64
                qkv = qkv.at[:, at : at + 128, j * 128 : (j + 1) * 128].set(pack[:384].reshape(3, 128, 128))
                out = out.at[hd : hd + 64, fr * 256 : fr * 256 + 128].set(pack[384:448])
                out = out.at[hd : hd + 64, fr * 256 + 128 : fr * 256 + 256].set(pack[448:512])
    return qkv, out


def local(
    tokens, gain_one, shift_one, w_qkv, w_attn_out, gain_two, shift_two, w_router, w_in, w_out, routes, cotangent
):
    nf, nh = lax.axis_size("fsdp"), lax.axis_size("heads")
    near = nf == 2 and nh == 4
    f, h, t = lax.axis_index("fsdp"), lax.axis_index("heads"), lax.axis_index("tensor")
    zero = jnp.zeros((), jnp.int32)
    idx = jnp.stack([f if near else zero, t % 2 if near else zero, t, h]).astype(jnp.int32)
    small_own = jnp.concatenate([w_router.T, jnp.stack([gain_one, shift_one, gain_two, shift_two])])

    if near:
        (pack,) = call(pack_kernel, [sds((512, 128), BF)], (idx, w_qkv, w_attn_out))
        pack = jnp.stack([pack, other(pack)])
        small_oth = other(small_own)
        small = jnp.where(
            f == 0, jnp.concatenate([small_own, small_oth], 1), jnp.concatenate([small_oth, small_own], 1)
        )
        packs = []
        for j in range(4):
            mine = flip(pack, "heads", j) if j else pack
            packs += [mine, core(mine)]
        weights = (w_in, other(w_in), w_out, other(w_out))
    else:
        small = lax.all_gather(small_own, "fsdp", axis=1, tiled=True)
        qkv_all = lax.all_gather(lax.all_gather(w_qkv, "fsdp", axis=1, tiled=True), "heads", axis=2, tiled=True)
        out_all = lax.all_gather(lax.all_gather(w_attn_out, "fsdp", axis=1, tiled=True), "heads", axis=0, tiled=True)
        packs = packs_of_whole(qkv_all, out_all)
        in_all = lax.all_gather(w_in, "fsdp", axis=1, tiled=True)
        o_all = lax.all_gather(w_out, "fsdp", axis=2, tiled=True)
        weights = (in_all[:, :256], in_all[:, 256:], o_all[:, :, :256], o_all[:, :, 256:])

    tok, cot0 = call(pad_kernel, [sds((ROWS, D), BF)] * 2, (idx, tokens, cotangent))
    cot1, cot2 = core(cot0), across(cot0)
    cot3 = core(cot2)
    sel = jnp.sum((routes[:, :, None] == jnp.arange(8, dtype=jnp.int32)).astype(F32), 1)
    sel = jnp.pad(sel.reshape(4, 2, SEQ, 8), ((0, 0), (0, 0), (0, PAD - SEQ), (0, 0))).reshape(4, ROWS, 8)

    n1, n2_0, resid, qkv, mix, wq, wo = call(
        attn_fwd_kernel,
        [
            sds((ROWS, D), BF),
            sds((ROWS, D), BF),
            sds((ROWS, D), F32),
            sds((4, ROWS, 384), BF),
            sds((4, ROWS, 128), BF),
            sds((4, D, 384), BF),
            sds((4, 128, D), BF),
        ],
        (idx, tok, small, *packs),
    )
    n2_1, n2_2 = core(n2_0), across(n2_0)
    n2_3 = core(n2_2)

    gin, gout, m0, m1, d0, d1, wr_a = moe(False, idx, (n2_0, n2_1), (cot0, cot1), sel, small, weights, ())
    keep, send, m2, m3, d2, d3, wr_b = moe(True, idx, (n2_2, n2_3), (cot2, cot3), sel, small, weights, (gin, gout))

    d_near, m_near = core(d1), core(m1)
    d_far = across(plus(d2, core(d3)).astype(BF))
    m_far = across(plus(m2, core(m3)).astype(BF))

    outs = call(
        attn_bwd_kernel,
        [sds((2, 512, 128), BF)] * 8 + [sds((SEQ * 2, D), BF), sds((8, D), F32)],
        (idx, d0, d_near, d_far, resid, cot0, tok, small, n1, qkv, mix, wq, wo, wr_a + wr_b),
        [
            pltpu.VMEM((ROWS, 384), BF),
            pltpu.VMEM((D, 384), BF),
            pltpu.VMEM((128, D), BF),
            pltpu.VMEM((ROWS, D), F32),
        ],
    )
    packs, input_grad, sgrad = outs[:8], outs[8], outs[9]
    (output,) = call(out_kernel, [sds((SEQ * 2, D), BF)], (idx, resid, m0, m_near, m_far))

    if near:
        totals = []
        for e in range(EXPERTS):
            part = plus(keep[e], other(send[e])).astype(BF)
            part = plus(part, lax.ppermute(part, "heads", [(0, 1), (3, 2)])).astype(BF)
            part = plus(part, lax.ppermute(part, "heads", [(1, 2), (2, 1)])).astype(BF)
            part = jnp.where((h == 0) | (h == 3), lax.ppermute(part, "heads", [(1, 0), (2, 3)]), part)
            totals.append(part)
        win_grad, wout_grad = finish(idx, jnp.stack(totals))

        halves = [plus(packs[2 * j], core(packs[2 * j + 1])).astype(BF) for j in range(4)]
        sgrad = sgrad + core(sgrad)
        half = plus(halves[0], *[flip(halves[j], "heads", j) for j in range(1, 4)]).astype(BF)
        pieces = [sgrad] + [flip(sgrad, "heads", j) for j in range(1, 4)]
        sgrad = (pieces[0] + pieces[1]) + (pieces[2] + pieces[3])
        half = plus(half[0], other(half[1])).astype(BF)
        sgrad = sgrad + other(sgrad)
        half = plus(half, across(half)).astype(BF)
        sgrad = sgrad + across(sgrad)
        qkv_grad, o_grad = call(
            unpack_kernel, [sds((3, 256, 128), F32), sds((128, 256), F32)], (idx, half, core(half))
        )
        sgrad = lax.dynamic_slice_in_dim(sgrad, f * 256, 256, 1)
    else:
        gin = jnp.concatenate([keep[:, :256], send[:, :256]], 1)
        gout = jnp.concatenate([keep[:, 256:], send[:, 256:]], 1).transpose(0, 2, 1)
        win_grad = lax.psum_scatter(gin, "fsdp", scatter_dimension=1, tiled=True)
        wout_grad = lax.psum_scatter(gout, "fsdp", scatter_dimension=2, tiled=True)
        win_grad = lax.psum(win_grad, "heads").astype(F32)
        wout_grad = lax.psum(wout_grad, "heads").astype(F32)
        qkv_grad, o_grad = whole_of_packs(packs)
        both = ("fsdp", "heads", "tensor")
        qkv_grad = lax.psum_scatter(qkv_grad, "fsdp", scatter_dimension=1, tiled=True)
        qkv_grad = lax.psum_scatter(qkv_grad, "heads", scatter_dimension=2, tiled=True)
        qkv_grad = lax.psum(qkv_grad, "tensor")
        o_grad = lax.psum_scatter(o_grad, "fsdp", scatter_dimension=1, tiled=True)
        o_grad = lax.psum_scatter(o_grad, "heads", scatter_dimension=0, tiled=True)
        o_grad = lax.psum(o_grad, "tensor")
        sgrad = lax.psum(sgrad, both)
        sgrad = lax.dynamic_slice_in_dim(sgrad, f * gain_one.shape[0], gain_one.shape[0], 1)

    return (
        output,
        input_grad,
        sgrad[4],
        sgrad[5],
        qkv_grad,
        o_grad,
        sgrad[6],
        sgrad[7],
        sgrad[0:4].T,
        win_grad,
        wout_grad,
    )


def solution(mesh):
    placed = (
        P(("fsdp", "heads", "tensor"), None),
        P("fsdp"),
        P("fsdp"),
        P(None, "fsdp", "heads"),
        P("heads", "fsdp"),
        P("fsdp"),
        P("fsdp"),
        P("fsdp", None),
        P(None, "fsdp", "tensor"),
        P(None, "tensor", "fsdp"),
        P(("fsdp", "heads"), None),
        P(("fsdp", "heads", "tensor"), None),
    )
    return jax.shard_map(
        local,
        mesh=mesh,
        in_specs=placed,
        out_specs=(
            P(("fsdp", "heads", "tensor"), None),
            P(("fsdp", "heads", "tensor"), None),
            P("fsdp"),
            P("fsdp"),
            P(None, "fsdp", "heads"),
            P("heads", "fsdp"),
            P("fsdp"),
            P("fsdp"),
            P("fsdp", None),
            P(None, "fsdp", "tensor"),
            P(None, "tensor", "fsdp"),
        ),
        check_vma=False,
    )
```

time: 927 us -> 334 us (0.36); the launches traced: 914 us -> 334 us
  local copies, waits for them, and re-layouts: 199 us -> 11.2 us
  blocking collectives: 187 us -> 0 us
  other arithmetic: 130 us -> 10.6 us
  waiting for transfers between devices: 293 us -> 178 us
  Pallas kernels: 0 us -> 78 us
  matrix products: 76.1 us -> 0 us
  starting transfers between devices: 11.5 us -> 54.1 us
  between operations: 17.7 us -> 1.27 us
    ppermute x0 -> x55, waiting for transfers between devices: none -> 178 us  [the longest x43 123 us: flip(): return lax.ppermute(x, axis, [(i, i ^ bit) for i in range(n)])]
    reduce_scatter x4 -> x0, waiting for transfers between devices: 171 us -> none  [the longest x1 87.2 us: local(): lax.psum_scatter(grad_inner, ('fsdp', 'heads'), scatter_dimension=1, tile...]
    unnamed x5 -> x0, blocking collectives: 136 us -> none
    all_gather x8 -> x0, waiting for transfers between devices: 95.2 us -> none  [the longest x1 35.4 us: local(): attended_grad = lax.all_gather(attn_grad_own, 'heads', axis=0, tiled=True)]
    pallas_call x0 -> x9, Pallas kernels: none -> 78 us  [the longest x2 41.1 us: moe(): pl.pallas_call(functools.partial(moe_kernel, final), grid=(EXPERTS,), out...]
    dot_general x20 -> x0, matrix products: 75 us -> none  [the longest x1 12.5 us: local(): jnp.einsum('ecd,edf->ecf', dispatched, inner_full, preferred_element_type...]
    reduce_sum x15 -> x1, other arithmetic: 59.9 us -> 0.01 us  [local(): jnp.sum((routes[:, :, None] == jnp.arange(8, dtype=jnp.int32)).astype(F32...]
    ppermute x0 -> x55, starting transfers between devices: none -> 54.1 us  [the longest x43 39.5 us: flip(): return lax.ppermute(x, axis, [(i, i ^ bit) for i in range(n)])]
  transfers between devices with their start and end apart: 19 -> 55, of which waited for: 7 -> 25; matrix products, arithmetic and copies ran while one was open for 35% -> 5% of each run, Pallas kernels for 0% -> 15%
where the time goes in v1:
time: 334 us
  waiting for transfers between devices  178 us (53%)
  Pallas kernels  78 us (23%)
  starting transfers between devices  54.1 us (16%)
  local copies, waits for them, and re-layouts  11.2 us (3%)
  other arithmetic  10.6 us (3%)
    ppermute x43, waiting for transfers between devices, flip(): return lax.ppermute(x, axis, [(i, i ^ bit) for i in range(n)])  123 us
    pallas_call x2, Pallas kernels, moe(): pl.pallas_call(functools.partial(moe_kernel, final), grid=(EXPERTS,), out...  41.1 us
    ppermute x43, starting transfers between devices, flip(): return lax.ppermute(x, axis, [(i, i ^ bit) for i in range(n)])  39.5 us
    ppermute x4, waiting for transfers between devices, local(): lax.ppermute(part, 'heads', [(1, 0), (2, 3)])  36.8 us
    pallas_call x6, Pallas kernels, call(): pl.pallas_call(kernel, out_shape=outs, in_specs=[smem()] + [vmem()] * (le...  32.7 us
    ppermute x4, waiting for transfers between devices, local(): part = plus(part, lax.ppermute(part, 'heads', [(0, 1), (3, 2)])).astype(BF)  18.6 us
  transfers between devices with their start and end apart: 55, of which 25 were waited for; matrix products, arithmetic and copies ran while one was open for 5% of the time, Pallas kernels for 15%

profile of v1, /device:TPU:0, one launch (start us, length us, event | category | flops | bytes accessed | tf_op | source)
XLA Modules:
  0.0 333.6 jit_solution(12795670886406278219)
XLA Ops:
  2.9 2.9 collective-permute-start.1
  5.8 3.7 %collective-permute-done.1 = bf16[512,128]{1,0:T(8,128)(2,1)S(1)} collective-permute-done((bf16[512,128]{1,0:T(8,128)(2,1)}, bf16[512,128]{1,0:T(8,128)(2,1)S(1)}, u32[]{:S(2)}, u32[]{:S(2)}) %collective-permute-start.1) | collective-permute-done | bytes 131104 | tf_op jit(solution)/shard_map/ppermute | solution.py:360
  10.5 3.9 %collective-permute-start.7 = (bf16[2,512,128]{2,1,0:T(8,128)(2,1)S(1)}, bf16[2,512,128]{2,1,0:T(8,128)(2,1)S(1)}, u32[]{:S(2)}, u32[]{:S(2)}) collective-permute-start(bf16[2,512,128]{2,1,0:T(8,128)(2,1)S(1)} %pad_maximum_fusion.1.refs_0_), channel_id=1, source_target_pairs={{0,12},{4,8},{8,4},{12,0},{1,13},{5,9},{9,5},{13,1},{2,14},{6,10},... | collective-permute-start | bytes 786440 | tf_op jit(solution)/shard_map/ppermute | solution.py:360
  15.1 6.7 %collective-permute-done.7.refs_6_ = bf16[2,512,128]{2,1,0:T(8,128)(2,1)S(1)} collective-permute-done((bf16[2,512,128]{2,1,0:T(8,128)(2,1)S(1)}, bf16[2,512,128]{2,1,0:T(8,128)(2,1)S(1)}, u32[]{:S(2)}, u32[]{:S(2)}) %collective-permute-start.7) | collective-permute-done | bytes 262176 | tf_op jit(solution)/shard_map/ppermute | solution.py:360
  21.7 14.1 %collective-permute-done.5.refs_4_ = bf16[2,512,128]{2,1,0:T(8,128)(2,1)S(1)} collective-permute-done((bf16[2,512,128]{2,1,0:T(8,128)(2,1)S(1)}, bf16[2,512,128]{2,1,0:T(8,128)(2,1)S(1)}, u32[]{:S(2)}, u32[]{:S(2)}) %collective-permute-start.5) | collective-permute-done | bytes 262176 | tf_op jit(solution)/shard_map/ppermute | solution.py:360
  49.7 9.4 %shard_map.205 = (bf16[416,512]{1,0:T(8,128)(2,1)}, bf16[416,512]{1,0:T(8,128)(2,1)}, f32[416,512]{1,0:T(8,128)}, bf16[4,416,384]{2,1,0:T(8,128)(2,1)}, bf16[4,4...) custom-call(s32[4]{0:T(128)} %pad_add_fusion.idx, ...), custom_call_target="tpu_custom_call" | custom-call | tf_op jit(solution)/shard_map/pallas_call | solution.py:52
  60.2 11.5 %collective-permute-done.14.x0 = bf16[416,512]{1,0:T(8,128)(2,1)} collective-permute-done((bf16[416,512]{1,0:T(8,128)(2,1)}, bf16[416,512]{1,0:T(8,128)(2,1)}, u32[]{:S(2)}, u32[]{:S(2)}) %collective-permute-start.14) | collective-permute-done | bytes 426016 | tf_op jit(solution)/shard_map/ppermute | solution.py:360
  73.2 16.9 %collective-permute-done.12.wout_b = bf16[4,512,256]{2,1,0:T(8,128)(2,1)S(1)} collective-permute-done((bf16[4,512,256]{2,1,0:T(8,128)(2,1)}, bf16[4,512,256]{2,1,0:T(8,128)(2,1)S(1)}, u32[]{:S(2)}, u32[]{:S(2)}) %collective-permute-start.12) | collective-permute-done | bytes 1048608 | tf_op jit(solution)/shard_map/ppermute | solution.py:360
  91.1 20.4 %shard_map.206 = (f32[4,512,512]{2,1,0:T(8,128)}, f32[4,512,512]{2,1,0:T(8,128)}, bf16[416,512]{1,0:T(8,128)(2,1)}, bf16[416,512]{1,0:T(8,128)(2,1)}, bf16[416,5...) custom-call(s32[4]{0:T(128)} %pad_add_fusion.idx, bf16[416,512]{1,0:T(8,128)(2,1)} %get-tuple-element.50.x0, ...), custom_call_target="tpu_custom_call" | custom-call | tf_op jit(solution)/shard_map/pallas_call | solution.py:319
  111.5 20.7 %shard_map.207 = (bf16[4,512,512]{2,1,0:T(8,128)(2,1)}, bf16[4,512,512]{2,1,0:T(8,128)(2,1)}, bf16[416,512]{1,0:T(8,128)(2,1)}, bf16[416,512]{1,0:T(8,128)(2,1)}...) custom-call(s32[4]{0:T(128)} %pad_add_fusion.idx, ...), custom_call_target="tpu_custom_call" | custom-call | tf_op jit(solution)/shard_map/pallas_call | solution.py:319
  136.9 2.8 slice_bitcast_fusion.3
  141.9 5.3 %collective-permute-done.22.d2 = bf16[416,512]{1,0:T(8,128)(2,1)S(1)} collective-permute-done((bf16[416,512]{1,0:T(8,128)(2,1)S(1)}, bf16[416,512]{1,0:T(8,128)(2,1)S(1)}, u32[]{:S(2)}, u32[]{:S(2)}) %collective-permute-start.22) | collective-permute-done | bytes 426016 | tf_op jit(solution)/shard_map/ppermute | solution.py:360
  148.0 15.2 %shard_map.209 = (bf16[2,512,128]{2,1,0:T(8,128)(2,1)}, bf16[2,512,128]{2,1,0:T(8,128)(2,1)}, bf16[2,512,128]{2,1,0:T(8,128)(2,1)}, bf16[2,512,128]{2,1,0:T(8,12...) custom-call(s32[4]{0:T(128)} %pad_add_fusion.idx, ...), custom_call_target="tpu_custom_call" | custom-call | tf_op jit(solution)/shard_map/pallas_call | solution.py:52
  177.1 29.7 %collective-permute-done.27 = f32[8,512]{1,0:T(8,128)S(1)} collective-permute-done((f32[8,512]{1,0:T(8,128)S(1)}, f32[8,512]{1,0:T(8,128)S(1)}, u32[]{:S(2)}, u32[]{:S(2)}) %collective-permute-start.27) | collective-permute-done | bytes 16416 | tf_op jit(solution)/shard_map/ppermute | solution.py:360
  224.9 11.1 %collective-permute-done.52 = bf16[512,512]{1,0:T(8,128)(2,1)S(1)} collective-permute-done((bf16[512,512]{1,0:T(8,128)(2,1)S(1)}, bf16[512,512]{1,0:T(8,128)(2,1)S(1)}, u32[]{:S(2)}, u32[]{:S(2)}) %collective-permute-start.52) | collective-permute-done | bytes 524320 | tf_op jit(solution)/shard_map/ppermute | solution.py:488
  241.4 5.8 %collective-permute-done.48 = bf16[512,512]{1,0:T(8,128)(2,1)S(1)} collective-permute-done((bf16[512,512]{1,0:T(8,128)(2,1)S(1)}, bf16[512,512]{1,0:T(8,128)(2,1)S(1)}, u32[]{:S(2)}, u32[]{:S(2)}) %collective-permute-start.48) | collective-permute-done | bytes 524320 | tf_op jit(solution)/shard_map/ppermute | solution.py:488
  250.4 13.6 %collective-permute-done.31 = bf16[2,512,128]{2,1,0:T(8,128)(2,1)S(1)} collective-permute-done((bf16[2,512,128]{2,1,0:T(8,128)(2,1)S(1)}, bf16[2,512,128]{2,1,0:T(8,128)(2,1)S(1)}, u32[]{:S(2)}, u32[]{:S(2)}) %collective-permute-start.31) | collective-permute-done | bytes 262176 | tf_op jit(solution)/shard_map/ppermute | solution.py:360
  264.8 5.0 %collective-permute-done.33 = bf16[2,512,128]{2,1,0:T(8,128)(2,1)S(1)} collective-permute-done((bf16[2,512,128]{2,1,0:T(8,128)(2,1)S(1)}, bf16[2,512,128]{2,1,0:T(8,128)(2,1)S(1)}, u32[]{:S(2)}, u32[]{:S(2)}) %collective-permute-start.33) | collective-permute-done | bytes 262176 | tf_op jit(solution)/shard_map/ppermute | solution.py:360
  270.4 5.0 %collective-permute-done.35 = bf16[2,512,128]{2,1,0:T(8,128)(2,1)S(1)} collective-permute-done((bf16[2,512,128]{2,1,0:T(8,128)(2,1)S(1)}, bf16[2,512,128]{2,1,0:T(8,128)(2,1)S(1)}, u32[]{:S(2)}, u32[]{:S(2)}) %collective-permute-start.35) | collective-permute-done | bytes 262176 | tf_op jit(solution)/shard_map/ppermute | solution.py:360
  290.7 8.5 %collective-permute-done.42 = bf16[512,512]{1,0:T(8,128)(2,1)S(1)} collective-permute-done((bf16[512,512]{1,0:T(8,128)(2,1)S(1)}, bf16[512,512]{1,0:T(8,128)(2,1)S(1)}, u32[]{:S(2)}, u32[]{:S(2)}) %collective-permute-start.42) | collective-permute-done | bytes 524320 | tf_op jit(solution)/shard_map/ppermute | solution.py:490
  299.3 11.2 %collective-permute-done.54 = bf16[512,512]{1,0:T(8,128)(2,1)S(1)} collective-permute-done((bf16[512,512]{1,0:T(8,128)(2,1)S(1)}, bf16[512,512]{1,0:T(8,128)(2,1)S(1)}, u32[]{:S(2)}, u32[]{:S(2)}) %collective-permute-start.54) | collective-permute-done | bytes 524320 | tf_op jit(solution)/shard_map/ppermute | solution.py:490
  310.5 11.2 %collective-permute-done.50 = bf16[512,512]{1,0:T(8,128)(2,1)S(1)} collective-permute-done((bf16[512,512]{1,0:T(8,128)(2,1)S(1)}, bf16[512,512]{1,0:T(8,128)(2,1)S(1)}, u32[]{:S(2)}, u32[]{:S(2)}) %collective-permute-start.50) | collective-permute-done | bytes 524320 | tf_op jit(solution)/shard_map/ppermute | solution.py:490
  321.7 6.0 %collective-permute-done.46 = bf16[512,512]{1,0:T(8,128)(2,1)S(1)} collective-permute-done((bf16[512,512]{1,0:T(8,128)(2,1)S(1)}, bf16[512,512]{1,0:T(8,128)(2,1)S(1)}, u32[]{:S(2)}, u32[]{:S(2)}) %collective-permute-start.46) | collective-permute-done | bytes 524320 | tf_op jit(solution)/shard_map/ppermute | solution.py:490
  329.3 4.3 %shard_map.211 = (f32[4,256,512]{2,1,0:T(8,128)}, f32[4,512,256]{2,1,0:T(8,128)}) custom-call(s32[4]{0:T(128)} %pad_add_fusion.idx, bf16[4,512,512]{2,1,0:T(8,128)(2,1)} %pad_maximum_fusion.total), custom_call_target="tpu_custom_call" | custom-call | tf_op jit(solution)/shard_map/pallas_call | solution.py:337
  (190 shorter events, 87.4 us)
Async XLA Ops:
  15.1 29.8 %collective-permute-start.2 = (bf16[2,512,128]{2,1,0:T(8,128)(2,1)S(1)}, bf16[2,512,128]{2,1,0:T(8,128)(2,1)S(1)}, u32[]{:S(2)}, u32[]{:S(2)}) collective-permute-start(bf16[2,512,128]{2,1,0:T(8,128)(2,1)S(1)} %pad_maximum_fusion.1.refs_0_), channel_id=1, source_target_pairs={{0,1},{1,0},{2,3},{3,2},{4,5},{5,4},{6,7},{7,6},{8,9},{9,8},{10,11... | collective-permute-start | bytes 786440 | tf_op jit(solution)/shard_map/ppermute | solution.py:360
  21.7 26.4 %collective-permute-start.8 = (bf16[2,512,128]{2,1,0:T(8,128)(2,1)S(1)}, bf16[2,512,128]{2,1,0:T(8,128)(2,1)}, u32[]{:S(2)}, u32[]{:S(2)}) collective-permute-start(bf16[2,512,128]{2,1,0:T(8,128)(2,1)S(1)} %collective-permute-done.7.refs_6_), channel_id=1, source_target_pairs={{0,1},{1,0},{2,3},{3,2},{4,5},{5,4},{6,7},{7,6},{8,9},{9,8},{10,11... | collective-permute-start | bytes 786440 | tf_op jit(solution)/shard_map/ppermute | solution.py:360
  43.4 29.8 %collective-permute-start.11 = (bf16[4,256,512]{2,1,0:T(8,128)(2,1)}, bf16[4,256,512]{2,1,0:T(8,128)(2,1)S(1)}, u32[]{:S(2)}, u32[]{:S(2)}) collective-permute-start(bf16[4,256,512]{2,1,0:T(8,128)(2,1)} %win_a.3), channel_id=1, source_target_pairs={{0,16},{16,0},{1,17},{17,1},{2,18},{18,2},{3,19},{19,3},{4,20},{20... | collective-permute-start | bytes 3145736 | tf_op jit(solution)/shard_map/ppermute | solution.py:360
  44.9 45.2 %collective-permute-start.12 = (bf16[4,512,256]{2,1,0:T(8,128)(2,1)}, bf16[4,512,256]{2,1,0:T(8,128)(2,1)S(1)}, u32[]{:S(2)}, u32[]{:S(2)}) collective-permute-start(bf16[4,512,256]{2,1,0:T(8,128)(2,1)} %wout_a.3), channel_id=1, source_target_pairs={{0,16},{16,0},{1,17},{17,1},{2,18},{18,2},{3,19},{19,3},{4,20},{20... | collective-permute-start | bytes 3145736 | tf_op jit(solution)/shard_map/ppermute | solution.py:360
  59.7 30.4 %collective-permute-start.9 = (bf16[416,512]{1,0:T(8,128)(2,1)}, bf16[416,512]{1,0:T(8,128)(2,1)}, u32[]{:S(2)}, u32[]{:S(2)}) collective-permute-start(bf16[416,512]{1,0:T(8,128)(2,1)} %get-tuple-element.50.x0), channel_id=1, source_target_pairs={{0,1},{1,0},{2,3},{3,2},{4,5},{5,4},{6,7},{7,6},{8,9},{9,8},{10,11... | collective-permute-start | bytes 1277960 | tf_op jit(solution)/shard_map/ppermute | solution.py:360
  59.9 51.6 %collective-permute-start.17 = (bf16[416,512]{1,0:T(8,128)(2,1)}, bf16[416,512]{1,0:T(8,128)(2,1)}, u32[]{:S(2)}, u32[]{:S(2)}) collective-permute-start(bf16[416,512]{1,0:T(8,128)(2,1)} %collective-permute-done.16.g0), channel_id=1, source_target_pairs={{0,1},{1,0},{2,3},{3,2},{4,5},{5,4},{6,7},{7,6},{8,9},{9,8},{10,11... | collective-permute-start | bytes 1277960 | tf_op jit(solution)/shard_map/ppermute | solution.py:360
  71.7 39.8 %collective-permute-start.15 = (bf16[416,512]{1,0:T(8,128)(2,1)}, bf16[416,512]{1,0:T(8,128)(2,1)}, u32[]{:S(2)}, u32[]{:S(2)}) collective-permute-start(bf16[416,512]{1,0:T(8,128)(2,1)} %collective-permute-done.14.x0), channel_id=1, source_target_pairs={{0,1},{1,0},{2,3},{3,2},{4,5},{5,4},{6,7},{7,6},{8,9},{9,8},{10,11... | collective-permute-start | bytes 1277960 | tf_op jit(solution)/shard_map/ppermute | solution.py:360
  139.7 35.0 %collective-permute-start.39 = (bf16[512,512]{1,0:T(8,128)(2,1)S(1)}, bf16[512,512]{1,0:T(8,128)(2,1)S(1)}, u32[]{:S(2)}, u32[]{:S(2)}) collective-permute-start(bf16[512,512]{1,0:T(8,128)(2,1)S(1)} %get-tuple-element.89), channel_id=1, source_target_pairs={{0,16},{16,0},{1,17},{17,1},{2,18},{18,2},{3,19},{19,3},{4,20},{20... | collective-permute-start | bytes 1572872 | tf_op jit(solution)/shard_map/ppermute | solution.py:360
  141.3 33.3 %collective-permute-start.18 = (bf16[416,512]{1,0:T(8,128)(2,1)S(1)}, bf16[416,512]{1,0:T(8,128)(2,1)S(1)}, u32[]{:S(2)}, u32[]{:S(2)}) collective-permute-start(bf16[416,512]{1,0:T(8,128)(2,1)S(1)} %copy-done.20), channel_id=1, source_target_pairs={{0,1},{1,0},{2,3},{3,2},{4,5},{5,4},{6,7},{7,6},{8,9},{9,8},{10,11... | collective-permute-start | bytes 1277960 | tf_op jit(solution)/shard_map/ppermute | solution.py:360
  171.0 37.4 %collective-permute-start.51 = (bf16[512,512]{1,0:T(8,128)(2,1)}, bf16[512,512]{1,0:T(8,128)(2,1)S(1)}, u32[]{:S(2)}, u32[]{:S(2)}) collective-permute-start(bf16[512,512]{1,0:T(8,128)(2,1)} %get-tuple-element.90), channel_id=1, source_target_pairs={{0,16},{16,0},{1,17},{17,1},{2,18},{18,2},{3,19},{19,3},{4,20},{20... | collective-permute-start | bytes 1572872 | tf_op jit(solution)/shard_map/ppermute | solution.py:360
  172.5 36.4 %collective-permute-start.47 = (bf16[512,512]{1,0:T(8,128)(2,1)}, bf16[512,512]{1,0:T(8,128)(2,1)}, u32[]{:S(2)}, u32[]{:S(2)}) collective-permute-start(bf16[512,512]{1,0:T(8,128)(2,1)} %get-tuple-element.91), channel_id=1, source_target_pairs={{0,16},{16,0},{1,17},{17,1},{2,18},{18,2},{3,19},{19,3},{4,20},{20... | collective-permute-start | bytes 1572872 | tf_op jit(solution)/shard_map/ppermute | solution.py:360
  174.1 34.9 %collective-permute-start.43 = (bf16[512,512]{1,0:T(8,128)(2,1)}, bf16[512,512]{1,0:T(8,128)(2,1)}, u32[]{:S(2)}, u32[]{:S(2)}) collective-permute-start(bf16[512,512]{1,0:T(8,128)(2,1)} %get-tuple-element.92), channel_id=1, source_target_pairs={{0,16},{16,0},{1,17},{17,1},{2,18},{18,2},{3,19},{19,3},{4,20},{20... | collective-permute-start | bytes 1572872 | tf_op jit(solution)/shard_map/ppermute | solution.py:360
  174.6 39.2 %collective-permute-start.13 = (bf16[416,512]{1,0:T(8,128)(2,1)}, bf16[416,512]{1,0:T(8,128)(2,1)}, u32[]{:S(2)}, u32[]{:S(2)}) collective-permute-start(bf16[416,512]{1,0:T(8,128)(2,1)} %get-tuple-element.53), channel_id=1, source_target_pairs={{0,1},{1,0},{2,3},{3,2},{4,5},{5,4},{6,7},{7,6},{8,9},{9,8},{10,11... | collective-permute-start | bytes 1277960 | tf_op jit(solution)/shard_map/ppermute | solution.py:360
  174.7 32.2 %collective-permute-start.27 = (f32[8,512]{1,0:T(8,128)S(1)}, f32[8,512]{1,0:T(8,128)S(1)}, u32[]{:S(2)}, u32[]{:S(2)}) collective-permute-start(f32[8,512]{1,0:T(8,128)S(1)} %add_add_fusion), channel_id=1, source_target_pairs={{0,16},{16,0},{1,17},{17,1},{2,18},{18,2},{3,19},{19,3},{4,20},{20... | collective-permute-start | bytes 49160 | tf_op jit(solution)/shard_map/ppermute | solution.py:360
  213.8 33.5 %collective-permute-start.48 = (bf16[512,512]{1,0:T(8,128)(2,1)S(1)}, bf16[512,512]{1,0:T(8,128)(2,1)S(1)}, u32[]{:S(2)}, u32[]{:S(2)}) collective-permute-start(bf16[512,512]{1,0:T(8,128)(2,1)S(1)} %get-tuple-element.87), channel_id=1, source_target_pairs={{0,4},{12,8},{1,5},{13,9},{2,6},{14,10},{3,7},{15,11},{16,20},{28,... | collective-permute-start | bytes 1572872 | tf_op jit(solution)/shard_map/ppermute | solution.py:488
  217.2 60.0 %collective-permute-start.44 = (bf16[512,512]{1,0:T(8,128)(2,1)S(1)}, bf16[512,512]{1,0:T(8,128)(2,1)S(1)}, u32[]{:S(2)}, u32[]{:S(2)}) collective-permute-start(bf16[512,512]{1,0:T(8,128)(2,1)S(1)} %get-tuple-element.88), channel_id=1, source_target_pairs={{0,4},{12,8},{1,5},{13,9},{2,6},{14,10},{3,7},{15,11},{16,20},{28,... | collective-permute-start | bytes 1572872 | tf_op jit(solution)/shard_map/ppermute | solution.py:488
  221.9 27.9 %collective-permute-start.29 = (bf16[2,512,128]{2,1,0:T(8,128)(2,1)S(1)}, bf16[2,512,128]{2,1,0:T(8,128)(2,1)S(1)}, u32[]{:S(2)}, u32[]{:S(2)}) collective-permute-start(bf16[2,512,128]{2,1,0:T(8,128)(2,1)S(1)} %copy-done.22), channel_id=1, source_target_pairs={{0,1},{1,0},{2,3},{3,2},{4,5},{5,4},{6,7},{7,6},{8,9},{9,8},{10,11... | collective-permute-start | bytes 786440 | tf_op jit(solution)/shard_map/ppermute | solution.py:360
  237.5 26.5 %collective-permute-start.31 = (bf16[2,512,128]{2,1,0:T(8,128)(2,1)S(1)}, bf16[2,512,128]{2,1,0:T(8,128)(2,1)S(1)}, u32[]{:S(2)}, u32[]{:S(2)}) collective-permute-start(bf16[2,512,128]{2,1,0:T(8,128)(2,1)S(1)} %add_convert_fusion.13), channel_id=1, source_target_pairs={{0,4},{4,0},{8,12},{12,8},{1,5},{5,1},{9,13},{13,9},{2,6},{6,2},{1... | collective-permute-start | bytes 786440 | tf_op jit(solution)/shard_map/ppermute | solution.py:360
  240.1 29.6 %collective-permute-start.33 = (bf16[2,512,128]{2,1,0:T(8,128)(2,1)S(1)}, bf16[2,512,128]{2,1,0:T(8,128)(2,1)S(1)}, u32[]{:S(2)}, u32[]{:S(2)}) collective-permute-start(bf16[2,512,128]{2,1,0:T(8,128)(2,1)S(1)} %add_convert_fusion.12), channel_id=1, source_target_pairs={{0,8},{4,12},{8,0},{12,4},{1,9},{5,13},{9,1},{13,5},{2,10},{6,14},... | collective-permute-start | bytes 786440 | tf_op jit(solution)/shard_map/ppermute | solution.py:360
  247.2 28.2 %collective-permute-start.35 = (bf16[2,512,128]{2,1,0:T(8,128)(2,1)S(1)}, bf16[2,512,128]{2,1,0:T(8,128)(2,1)S(1)}, u32[]{:S(2)}, u32[]{:S(2)}) collective-permute-start(bf16[2,512,128]{2,1,0:T(8,128)(2,1)S(1)} %add_convert_fusion.11), channel_id=1, source_target_pairs={{0,12},{4,8},{8,4},{12,0},{1,13},{5,9},{9,5},{13,1},{2,14},{6,10},... | collective-permute-start | bytes 786440 | tf_op jit(solution)/shard_map/ppermute | solution.py:360
  249.7 32.6 %collective-permute-start.41 = (bf16[512,512]{1,0:T(8,128)(2,1)S(1)}, bf16[512,512]{1,0:T(8,128)(2,1)S(1)}, u32[]{:S(2)}, u32[]{:S(2)}) collective-permute-start(bf16[512,512]{1,0:T(8,128)(2,1)S(1)} %add_convert_fusion.7), channel_id=1, source_target_pairs={{4,8},{8,4},{5,9},{9,5},{6,10},{10,6},{7,11},{11,7},{20,24},{24,20... | collective-permute-start | bytes 1572872 | tf_op jit(solution)/shard_map/ppermute | solution.py:489
  283.9 26.5 %collective-permute-start.54 = (bf16[512,512]{1,0:T(8,128)(2,1)S(1)}, bf16[512,512]{1,0:T(8,128)(2,1)S(1)}, u32[]{:S(2)}, u32[]{:S(2)}) collective-permute-start(bf16[512,512]{1,0:T(8,128)(2,1)S(1)} %add_convert_fusion), channel_id=1, source_target_pairs={{4,0},{8,12},{5,1},{9,13},{6,2},{10,14},{7,3},{11,15},{20,16},{24,... | collective-permute-start | bytes 1572872 | tf_op jit(solution)/shard_map/ppermute | solution.py:490
  285.3 36.3 %collective-permute-start.50 = (bf16[512,512]{1,0:T(8,128)(2,1)S(1)}, bf16[512,512]{1,0:T(8,128)(2,1)S(1)}, u32[]{:S(2)}, u32[]{:S(2)}) collective-permute-start(bf16[512,512]{1,0:T(8,128)(2,1)S(1)} %add_convert_fusion.2), channel_id=1, source_target_pairs={{4,0},{8,12},{5,1},{9,13},{6,2},{10,14},{7,3},{11,15},{20,16},{24,... | collective-permute-start | bytes 1572872 | tf_op jit(solution)/shard_map/ppermute | solution.py:490
  286.9 40.8 %collective-permute-start.46 = (bf16[512,512]{1,0:T(8,128)(2,1)S(1)}, bf16[512,512]{1,0:T(8,128)(2,1)S(1)}, u32[]{:S(2)}, u32[]{:S(2)}) collective-permute-start(bf16[512,512]{1,0:T(8,128)(2,1)S(1)} %add_convert_fusion.4), channel_id=1, source_target_pairs={{4,0},{8,12},{5,1},{9,13},{6,2},{10,14},{7,3},{11,15},{20,16},{24,... | collective-permute-start | bytes 1572872 | tf_op jit(solution)/shard_map/ppermute | solution.py:490
  (57 other events, 792.6 us)

commit v2 on v1

v2 whole, which is shorter than its diff:
```python
import functools

import jax
import jax.numpy as jnp
from jax import lax
from jax.experimental import pallas as pl
from jax.experimental.pallas import tpu as pltpu
from jax.sharding import PartitionSpec as P

HD = 64
SEQ = 197
PAD = 208
ROWS = 2 * PAD
D = 512
FFT = 512
EXPERTS = 4
BF = jnp.bfloat16
F32 = jnp.float32
PACK = 528
GELU_C = 0.7978845608028654


def nn(a, b):
    return lax.dot_general(a, b, (((1,), (0,)), ((), ())), preferred_element_type=F32)


def nt(a, b):
    return lax.dot_general(a, b, (((1,), (1,)), ((), ())), preferred_element_type=F32)


def tn(a, b):
    return lax.dot_general(a, b, (((0,), (0,)), ((), ())), preferred_element_type=F32)


def params(sem=None, mib=24):
    return pltpu.CompilerParams(vmem_limit_bytes=mib * 1024 * 1024, dimension_semantics=sem)


def smem():
    return pl.BlockSpec(memory_space=pltpu.SMEM)


def vmem():
    return pl.BlockSpec(memory_space=pltpu.VMEM)


def sds(shape, dtype):
    return jax.ShapeDtypeStruct(shape, dtype)


def skip(kernel, n_args, n_after):
    def run(*refs):
        kernel(*refs[:n_args], *refs[n_args + n_after :])

    return run


def call(kernel, outs, args, scratch=(), after=(), mib=24):
    return pl.pallas_call(
        skip(kernel, len(args), len(after)),
        out_shape=outs,
        in_specs=[smem()] + [vmem()] * (len(args) - 1) + [pl.BlockSpec(memory_space=pl.ANY)] * len(after),
        out_specs=[vmem()] * len(outs),
        scratch_shapes=list(scratch),
        compiler_params=params(mib=mib),
    )(*args, *after)


def pack_kernel(idx, wqkv, wo, wr, g1, s1, g2, s2, out):
    c = idx[1]
    rows = pl.ds(pl.multiple_of(c * 128, 128), 128)
    for i in range(3):
        out[i * 128 : (i + 1) * 128, :] = wqkv[i, rows, :]
    head = pl.ds(pl.multiple_of(c * 64, 64), 64)
    out[384:448, :] = wo[head, 0:128]
    out[448:512, :] = wo[head, 128:256]
    small = [wr[...].astype(F32).T] + [r[...].reshape(1, 256).astype(F32) for r in (g1, s1, g2, s2)]
    small = jnp.concatenate(small, axis=0).astype(BF)
    out[512:520, :] = small[:, 0:128]
    out[520:528, :] = small[:, 128:256]


def pair_kernel(idx, own, oth, out):
    out[0] = own[...]
    out[1] = oth[...]


def weights_kernel(idx, win, wout, out):
    for e in range(EXPERTS):
        out[e, 0:256, :] = win[e]
        out[e, 256:512, 0:256] = wout[e, 0:256, :]
        out[e, 256:512, 256:512] = wout[e, 256:512, :]


def spread(v):
    zero = jnp.zeros((PAD - SEQ, v.shape[1]), v.dtype)
    return jnp.concatenate([v[:SEQ], zero, v[SEQ:], zero], axis=0)


def close(v):
    return jnp.concatenate([v[:SEQ], v[PAD : PAD + SEQ]], axis=0)


def pad_kernel(idx, tok, cot, tok_out, cot_out):
    tok_out[...] = spread(tok[...].astype(F32)).astype(BF)
    cot_out[...] = spread(cot[...].astype(F32)).astype(BF)


def norm_parts(x):
    center = jnp.mean(x, -1, keepdims=True)
    centered = x - center
    rstd = lax.rsqrt(jnp.mean(centered * centered, -1, keepdims=True) + 1e-06)
    return centered * rstd, rstd


def norm_back(xhat, rstd, grad, gain):
    dxhat = grad * gain
    m1 = jnp.mean(dxhat, -1, keepdims=True)
    m2 = jnp.mean(dxhat * xhat, -1, keepdims=True)
    return rstd * (dxhat - m1 - xhat * m2)


def attn_fwd_kernel(first, idx, tok, *refs):
    packs, refs = refs[:4], refs[4:]
    if first:
        small, n1_ref, acc_ref, qkv_ref, mix_ref, wq_ref, wo_ref = refs
    else:
        small, n1_ref, acc_in, n2_ref, acc_ref, qkv_ref, mix_ref, wq_ref, wo_ref = refs
    f, c = idx[0], idx[1]
    if first:
        for fr in range(2):
            at = jnp.bitwise_xor(f, fr) * 256
            for i in range(2):
                cols = pl.ds(pl.multiple_of(at + i * 128, 128), 128)
                small[:, cols] = packs[0][fr, 512 + 8 * i : 520 + 8 * i, :]
        x = tok[...].astype(F32)
        xhat, _ = norm_parts(x)
        n1 = (xhat * small[4:5, :].astype(F32) + small[5:6, :].astype(F32)).astype(BF)
        n1_ref[...] = n1
        acc = [x[0:PAD], x[PAD:ROWS]]
    else:
        n1 = n1_ref[...]
        acc = [acc_in[0:PAD, :], acc_in[PAD:ROWS, :]]
    lane = lax.broadcasted_iota(jnp.int32, (PAD, 128), 1)
    key = lax.broadcasted_iota(jnp.int32, (PAD, PAD), 1)
    for j in range(2):
        for fr in range(2):
            fa = jnp.bitwise_xor(f, fr)
            for cr in range(2):
                ca = jnp.bitwise_xor(c, cr)
                src = packs[2 * j + cr]
                rows = pl.ds(pl.multiple_of(fa * 256 + ca * 128, 128), 128)
                for i in range(3):
                    wq_ref[j, rows, i * 128 : (i + 1) * 128] = src[fr, i * 128 : (i + 1) * 128, :]
                head = pl.ds(pl.multiple_of(ca * 64, 64), 64)
                for i in range(2):
                    cols = pl.ds(pl.multiple_of(fa * 256 + i * 128, 128), 128)
                    wo_ref[j, head, cols] = src[fr, 384 + 64 * i : 448 + 64 * i, :]
        qkv_ref[j] = nn(n1, wq_ref[j]).astype(BF)
        for im in range(2):
            r = slice(im * PAD, (im + 1) * PAD)
            q, k, v = (qkv_ref[j, r, i * 128 : (i + 1) * 128] for i in range(3))
            outs = []
            for head in range(2):
                s = nt(jnp.where(lane // HD == head, q, jnp.zeros_like(q)), k) * 0.125
                s = jnp.where(key < SEQ, s, -1e30)
                e = jnp.exp(s - jnp.max(s, -1, keepdims=True))
                p = e / jnp.sum(e, -1, keepdims=True)
                outs.append(nn(p.astype(BF), v))
            mix = jnp.where(lane < HD, outs[0], outs[1]).astype(BF)
            mix_ref[j, r, :] = mix
            acc[im] = acc[im] + nn(mix, wo_ref[j])
    for im in range(2):
        r = slice(im * PAD, (im + 1) * PAD)
        acc_ref[r, :] = acc[im]
        if not first:
            xhat, _ = norm_parts(acc[im])
            n2_ref[r, :] = (xhat * small[6:7, :].astype(F32) + small[7:8, :].astype(F32)).astype(BF)


def attn_bwd_kernel(
    idx, d0, d1, d2, resid, cot, tok, small, n1, qkv_a, qkv_b, mix_a, mix_b, wq_a, wq_b, wo_a, wo_b, wr_a, wr_b, *refs
):
    own, sib, igrad, dqkv_s, gq_s, go_s, dn1_s, sgrad = refs
    f, c = idx[0], idx[1]
    dn2 = d0[...].astype(F32) + d1[...].astype(F32) + d2[...].astype(F32)
    xhat, rstd = norm_parts(resid[...])
    sgrad[0:4, :] = (wr_a[...] + wr_b[...])[0:4]
    sgrad[6:7, :] = jnp.sum(dn2 * xhat, 0, keepdims=True)
    sgrad[7:8, :] = jnp.sum(dn2, 0, keepdims=True)
    dresid = cot[...].astype(F32) + norm_back(xhat, rstd, dn2, small[6:7, :].astype(F32))
    dattn = dresid.astype(BF)
    lane = lax.broadcasted_iota(jnp.int32, (PAD, 128), 1)
    key = lax.broadcasted_iota(jnp.int32, (PAD, PAD), 0)
    n1t = n1[...].T
    for j in range(4):
        qkv, mix, wq, wo = (pair[j // 2].at[j % 2] for pair in ((qkv_a, qkv_b), (mix_a, mix_b), (wq_a, wq_b), (wo_a, wo_b)))
        go_s[...] = tn(mix[...], dattn).astype(BF)
        dmix = nt(dattn, wo[...]).astype(BF)
        for im in range(2):
            r = slice(im * PAD, (im + 1) * PAD)
            q, k, v = (qkv[r, i * 128 : (i + 1) * 128] for i in range(3))
            dm = dmix[r]
            dq, dk, dv = [], [], []
            for head in range(2):
                keep = lane // HD == head
                s = nt(k, jnp.where(keep, q, jnp.zeros_like(q))) * 0.125
                s = jnp.where(key < SEQ, s, -1e30)
                e = jnp.exp(s - jnp.max(s, 0, keepdims=True))
                p = e / jnp.sum(e, 0, keepdims=True)
                dp = nt(v, jnp.where(keep, dm, jnp.zeros_like(dm)))
                ds = (p * (dp - jnp.sum(p * dp, 0, keepdims=True))).astype(BF)
                dq.append(tn(ds, k))
                dk.append(nn(ds, q))
                dv.append(nn(p.astype(BF), dm))
            first = lane < HD
            dqkv_s[r, 0:128] = (jnp.where(first, dq[0], dq[1]) * 0.125).astype(BF)
            dqkv_s[r, 128:256] = (jnp.where(first, dk[0], dk[1]) * 0.125).astype(BF)
            dqkv_s[r, 256:384] = jnp.where(first, dv[0], dv[1]).astype(BF)
        dqkv = dqkv_s[...]
        gq_s[...] = nn(n1t, dqkv).astype(BF)
        part = nt(dqkv, wq[...])
        if j == 0:
            dn1_s[...] = part
        else:
            dn1_s[...] += part
        for fr in range(2):
            fa = jnp.bitwise_xor(f, fr)
            for cr in range(2):
                ca = jnp.bitwise_xor(c, cr)
                dst = (own, sib)[cr]
                rows = pl.ds(pl.multiple_of(fa * 256 + ca * 128, 128), 128)
                for i in range(3):
                    dst[j, fr, i * 128 : (i + 1) * 128, :] = gq_s[rows, i * 128 : (i + 1) * 128]
                head = pl.ds(pl.multiple_of(ca * 64, 64), 64)
                for i in range(2):
                    cols = pl.ds(pl.multiple_of(fa * 256 + i * 128, 128), 128)
                    dst[j, fr, 384 + 64 * i : 448 + 64 * i, :] = go_s[head, cols]
    dn1 = dn1_s[...]
    xhat, rstd = norm_parts(tok[...].astype(F32))
    sgrad[4:5, :] = jnp.sum(dn1 * xhat, 0, keepdims=True)
    sgrad[5:6, :] = jnp.sum(dn1, 0, keepdims=True)
    for fr in range(2):
        for cr in range(2):
            at = jnp.bitwise_xor(f, fr) * 256 + jnp.bitwise_xor(c, cr) * 128
            rows = sgrad[:, pl.ds(pl.multiple_of(at, 128), 128)]
            rows = jnp.concatenate([rows, jnp.zeros_like(rows)], axis=0).astype(BF)
            for j in range(4):
                (own, sib)[cr][j, fr, 512:528, :] = rows
    grad = dresid + norm_back(xhat, rstd, dn1, small[4:5, :].astype(F32))
    igrad[...] = close(grad).astype(BF)


def out_kernel(idx, resid, m0, m1, m2, out):
    total = resid[...] + m0[...].astype(F32) + m1[...].astype(F32) + m2[...].astype(F32)
    out[...] = close(total).astype(BF)


def moe_kernel(start, end, final, base, e0, n, idx, x0, x1, g0, g1, routes, small, w_own, w_oth, *refs):
    take = lambda k: (refs[:k], refs[k:])
    if final:
        (gin_in, gout_in), refs = take(2)
    if not start:
        (mix_in, dn_in, dp_in), refs = take(3)
    if final:
        keeps, refs = take(n)
        sends, refs = take(n)
    else:
        (gin_out, gout_out), refs = take(2)
    if end:
        (mix0, mix1, dn0, dn1, wrg), refs = take(5)
    else:
        (mix_s, dn_s, dprob), refs = take(3)
    (win, wout, xt, gt, gates, router, chosen, gin_s, gout_s), refs = take(9)
    if end:
        mix_s, dn_s, dprob = refs
    step = pl.program_id(0)
    e = step + e0
    f, t = idx[0], idx[2]
    xs, gs = (x0, x1), (g0, g1)
    lane = lax.broadcasted_iota(jnp.int32, (ROWS, 8), 1)

    @pl.when(step == 0)
    def _():
        if start:
            dprob[...] = jnp.zeros_like(dprob)
            mix_s[...] = jnp.zeros_like(mix_s)
            dn_s[...] = jnp.zeros_like(dn_s)
        else:
            dprob[...] = dp_in[...]
            mix_s[...] = mix_in[...]
            dn_s[...] = dn_in[...]
        for b in range(2):
            xt[b] = xs[b][...].T
            gt[b] = gs[b][...].T
            logits = nt(xs[b][...], small[...])
            logits = jnp.where(lane < EXPERTS, logits, -1e30)
            ex = jnp.exp(logits - jnp.max(logits, -1, keepdims=True))
            prob = ex / jnp.sum(ex, -1, keepdims=True)
            router[b] = prob
            named = routes[jnp.bitwise_xor(t, base + b)]
            expert = lax.broadcasted_iota(jnp.int32, (8, ROWS), 0)
            hit = jnp.where((named[0:1] == expert) | (named[1:2] == expert), 1.0, 0.0).T
            chosen[b] = hit
            gates[b] = prob * hit

    own = pl.ds(pl.multiple_of(f * 256, 256), 256)
    oth = pl.ds(pl.multiple_of((1 - f) * 256, 256), 256)
    for w, half in ((w_own, own), (w_oth, oth)):
        win[half, :] = w[0, 0:256, :]
        wout[0:256, half] = w[0, 256:512, 0:256]
        wout[256:512, half] = w[0, 256:512, 256:512]
    gin = gout = None
    for b in range(2):
        inner = nn(xs[b][...], win[...])
        back = nt(gs[b][...], wout[...])
        gate = jnp.sum(jnp.where(lane == e, gates[b], 0.0), -1, keepdims=True)
        square = inner * inner
        th = jnp.tanh(GELU_C * inner * (1.0 + 0.044715 * square))
        half = 0.5 * (1.0 + th)
        hidden = inner * half
        slope = half + 0.5 * inner * (1.0 - th * th) * (GELU_C * (1.0 + (3 * 0.044715) * square))
        dprob[b] += jnp.where(lane == e, jnp.sum(hidden * back, -1, keepdims=True), 0.0)
        hg = (gate * hidden).astype(BF)
        di = (gate * back * slope).astype(BF)
        mix_s[b] += nn(hg, wout[...])
        dn_s[b] += nt(di, win[...])
        part_in, part_out = nn(xt[b], di), nn(gt[b], hg)
        gin = part_in if gin is None else gin + part_in
        gout = part_out if gout is None else gout + part_out
    if final:
        gin_s[...] = (gin + gin_in[0]).astype(BF)
        gout_s[...] = (gout + gout_in[0]).astype(BF)
        for i in range(n):

            @pl.when(step == i)
            def _():
                for dst, rows in ((keeps[i], own), (sends[i], oth)):
                    dst[0:256, :] = gin_s[rows, :]
                    dst[256:512, :] = gout_s[rows, :]
    else:
        gin_out[0] = gin
        gout_out[0] = gout
    if end:

        @pl.when(step == n - 1)
        def _():
            for b, dn, mx in ((0, dn0, mix0), (1, dn1, mix1)):
                dp = dprob[b] * chosen[b]
                dl = router[b] * (dp - jnp.sum(router[b] * dp, -1, keepdims=True))
                dl = jnp.where(lane < EXPERTS, dl, 0.0).astype(BF)
                dn[...] = (dn_s[b] + nn(dl, small[...])).astype(BF)
                mx[...] = mix_s[b].astype(BF)
                part = tn(dl, xs[b][...])
                if b == 0:
                    wrg[...] = part
                else:
                    wrg[...] += part


def moe(base, e0, n, idx, xs, gs, routes, small, weights, grads=(), sums=(), end=True, after=()):
    start, final = not sums, bool(grads)
    whole = lambda shape: pl.BlockSpec(shape, lambda e: (0,) * len(shape))
    expert = lambda at: pl.BlockSpec((1, 512, 512), lambda e: (e + at, 0, 0))
    row, both = whole((ROWS, D)), whole((2, ROWS, D))
    carry = [(2, ROWS, D), (2, ROWS, D), (2, ROWS, 8)]
    in_specs = [smem(), row, row, row, row, whole((4, 2, ROWS)), whole((8, D))] + [expert(e0)] * 2
    in_specs += [expert(e0)] * len(grads) + [whole(shape) for shape in carry[: len(sums)]]
    in_specs += [pl.BlockSpec(memory_space=pl.ANY)] * len(after)
    if final:
        outs, out_specs = [sds((512, 512), BF)] * (2 * n), [whole((512, 512))] * (2 * n)
    else:
        outs, out_specs = [sds((n, D, FFT), F32)] * 2, [expert(0)] * 2
    if end:
        outs += [sds((ROWS, D), BF)] * 4 + [sds((8, D), F32)]
        out_specs += [row] * 4 + [whole((8, D))]
    else:
        outs += [sds(shape, F32) for shape in carry]
        out_specs += [whole(shape) for shape in carry]
    scratch = [
        pltpu.VMEM((D, FFT), BF),
        pltpu.VMEM((FFT, D), BF),
        pltpu.VMEM((2, D, ROWS), BF),
        pltpu.VMEM((2, D, ROWS), BF),
        pltpu.VMEM((2, ROWS, 8), F32),
        pltpu.VMEM((2, ROWS, 8), F32),
        pltpu.VMEM((2, ROWS, 8), F32),
        pltpu.VMEM((D, FFT), BF),
        pltpu.VMEM((D, FFT), BF),
    ]
    if end:
        scratch += [pltpu.VMEM(shape, F32) for shape in carry]
    kernel = functools.partial(moe_kernel, start, end, final, base, e0, n)
    n_in = 9 + len(grads) + len(sums)
    return pl.pallas_call(
        skip(kernel, n_in, len(after)),
        grid=(n,),
        out_shape=outs,
        in_specs=in_specs,
        out_specs=out_specs,
        scratch_shapes=scratch,
        compiler_params=params(("arbitrary",), 44),
    )(idx, *xs, *gs, routes, small, *weights, *grads, *sums, *after)


def add_kernel(idx, a, b, out):
    out[...] = (a[...].astype(F32) + b[...].astype(F32)).astype(BF)


def add(idx, a, b, after=()):
    return call(add_kernel, [sds(a.shape, BF)], (idx, a, b), after=after)[0]


def finish_kernel(idx, mine, given, *refs):
    win_grad, wout_grad = refs[-2:]
    ends = (idx[3] == 0) | (idx[3] == 3)
    total = jnp.where(ends, given[...], mine[...]).astype(F32)
    win_grad[0] = total[0:256, :]
    wout_grad[0] = total[256:512, :].T


def finish(idx, e, mine, given, into=(), after=()):
    block = lambda shape: pl.BlockSpec((1,) + shape, lambda i: (e, 0, 0))
    anywhere = [pl.BlockSpec(memory_space=pl.ANY)]
    return pl.pallas_call(
        skip(finish_kernel, 3, len(into) + len(after)),
        grid=(1,),
        out_shape=[sds((EXPERTS, 256, FFT), F32), sds((EXPERTS, FFT, 256), F32)],
        in_specs=[smem(), vmem(), vmem()] + anywhere * (len(into) + len(after)),
        out_specs=[block((256, FFT)), block((FFT, 256))],
        input_output_aliases={3: 0, 4: 1} if into else {},
        compiler_params=params(),
    )(idx, mine, given, *into, *after)


def merge_kernel(idx, own, sib, *outs):
    for j in range(4):
        outs[j][...] = (own[j].astype(F32) + sib[j].astype(F32)).astype(BF)


def gather_kernel(idx, a, b, c, d, keep, send):
    total = ((a[...].astype(F32) + b[...].astype(F32)) + (c[...].astype(F32) + d[...].astype(F32))).astype(BF)
    keep[...] = total[0]
    send[...] = total[1]


def unpack_kernel(idx, own, sib, qkv_grad, o_grad, sgrad):
    c = idx[1]
    for src, ca in ((own, c), (sib, 1 - c)):
        rows = pl.ds(pl.multiple_of(ca * 128, 128), 128)
        for i in range(3):
            qkv_grad[i, rows, :] = src[i * 128 : (i + 1) * 128, :].astype(F32)
        head = pl.ds(pl.multiple_of(ca * 64, 64), 64)
        o_grad[head, 0:128] = src[384:448, :].astype(F32)
        o_grad[head, 128:256] = src[448:512, :].astype(F32)
        sgrad[:, rows] = src[512:520, :].astype(F32)


def flip(x, axis, bit):
    n = lax.axis_size(axis)
    return lax.ppermute(x, axis, [(i, i ^ bit) for i in range(n)])


def core(x):
    return flip(x, "tensor", 1)


def across(x):
    return flip(x, "tensor", 2)


def other(x):
    return flip(x, "fsdp", 1)


def packs_of_whole(qkv, out, small):
    packs = []
    for j in range(4):
        for cr in range(2):
            pair = []
            for fr in range(2):
                at = fr * 256 + cr * 128
                head = out[j * 128 + cr * 64 : j * 128 + cr * 64 + 64, fr * 256 : fr * 256 + 256]
                pair.append(
                    jnp.concatenate(
                        [qkv[i, at : at + 128, j * 128 : (j + 1) * 128] for i in range(3)]
                        + [head[:, :128], head[:, 128:]]
                        + [small[:, fr * 256 : fr * 256 + 128], small[:, fr * 256 + 128 : fr * 256 + 256]]
                    )
                )
            packs.append(jnp.stack(pair))
    return packs


def whole_of_packs(packs):
    qkv, out, small = jnp.zeros((3, D, D), F32), jnp.zeros((D, D), F32), jnp.zeros((8, D), F32)
    for j in range(4):
        for cr in range(2):
            for fr in range(2):
                pack = packs[cr][j, fr].astype(F32)
                at, hd = fr * 256 + cr * 128, j * 128 + cr * 64
                qkv = qkv.at[:, at : at + 128, j * 128 : (j + 1) * 128].set(pack[:384].reshape(3, 128, 128))
                out = out.at[hd : hd + 64, fr * 256 : fr * 256 + 128].set(pack[384:448])
                out = out.at[hd : hd + 64, fr * 256 + 128 : fr * 256 + 256].set(pack[448:512])
                small = small.at[:, at : at + 128].set(pack[512:520])
    return qkv, out, small


def local(
    tokens, gain_one, shift_one, w_qkv, w_attn_out, gain_two, shift_two, w_router, w_in, w_out, routes, cotangent
):
    nf, nh = lax.axis_size("fsdp"), lax.axis_size("heads")
    near = nf == 2 and nh == 4
    f, h, t = lax.axis_index("fsdp"), lax.axis_index("heads"), lax.axis_index("tensor")
    zero = jnp.zeros((), jnp.int32)
    idx = jnp.stack([f if near else zero, t % 2 if near else zero, t, h]).astype(jnp.int32)
    shapes = lambda *given: [sds(shape, dtype) for shape, dtype in given]

    if near:
        (pack,) = call(
            pack_kernel,
            [sds((PACK, 128), BF)],
            (idx, w_qkv, w_attn_out, w_router, gain_one, shift_one, gain_two, shift_two),
        )
        pack_far = other(pack)
        (w_own,) = call(weights_kernel, [sds((EXPERTS, 512, 512), BF)], (idx, w_in, w_out), after=(pack,))
        w_oth = other(w_own)
        tok, cot0 = call(pad_kernel, [sds((ROWS, D), BF)] * 2, (idx, tokens, cotangent), after=(w_own,))
        (pair,) = call(pair_kernel, [sds((2, PACK, 128), BF)], (idx, pack, pack_far), after=(tok,))
        packs = []
        for j in range(4):
            mine = flip(pair, "heads", j) if j else pair
            packs += [mine, core(mine)]
    else:
        small_own = jnp.concatenate([w_router.T, jnp.stack([gain_one, shift_one, gain_two, shift_two])])
        small = lax.all_gather(small_own, "fsdp", axis=1, tiled=True)
        qkv_all = lax.all_gather(lax.all_gather(w_qkv, "fsdp", axis=1, tiled=True), "heads", axis=2, tiled=True)
        out_all = lax.all_gather(lax.all_gather(w_attn_out, "fsdp", axis=1, tiled=True), "heads", axis=0, tiled=True)
        packs = packs_of_whole(qkv_all, out_all, small)
        in_all = lax.all_gather(w_in, "fsdp", axis=1, tiled=True)
        o_all = lax.all_gather(w_out, "fsdp", axis=2, tiled=True)
        (w_own,) = call(weights_kernel, [sds((EXPERTS, 512, 512), BF)], (idx, in_all[:, :256], o_all[:, :, :256]))
        (w_oth,) = call(weights_kernel, [sds((EXPERTS, 512, 512), BF)], (idx, in_all[:, 256:], o_all[:, :, 256:]))
        tok, cot0 = call(pad_kernel, [sds((ROWS, D), BF)] * 2, (idx, tokens, cotangent))

    named = jnp.pad(routes.T.reshape(2, 8, SEQ), ((0, 0), (0, 0), (0, PAD - SEQ)), constant_values=-1)
    named = named.reshape(2, 4, ROWS).transpose(1, 0, 2)

    kept = [((2, ROWS, 384), BF), ((2, ROWS, 128), BF), ((2, D, 384), BF), ((2, 128, D), BF)]
    small, n1, acc, qkv_a, mix_a, wq_a, wo_a = call(
        functools.partial(attn_fwd_kernel, True),
        shapes(((8, D), BF), ((ROWS, D), BF), ((ROWS, D), F32), *kept),
        (idx, tok, *packs[:4]),
    )
    cot1, cot2 = core(cot0), across(cot0)
    cot3 = core(cot2)
    n2_0, resid, qkv_b, mix_b, wq_b, wo_b = call(
        functools.partial(attn_fwd_kernel, False),
        shapes(((ROWS, D), BF), ((ROWS, D), F32), *kept),
        (idx, tok, *packs[4:], small, n1, acc),
    )
    n2_1, n2_2 = core(n2_0), across(n2_0)
    n2_3 = core(n2_2)

    shared = (named, small, (w_own, w_oth))
    gin, gout, m0, m1, d0, d1, wr_a = moe(0, 0, EXPERTS, idx, (n2_0, n2_1), (cot0, cot1), *shared)
    far = ((n2_2, n2_3), (cot2, cot3))
    keep0, send0, *sums = moe(2, 0, 1, idx, *far, *shared, grads=(gin, gout), end=False)
    outs = moe(2, 1, 3, idx, *far, *shared, grads=(gin, gout), sums=tuple(sums))
    keeps, sends = [keep0, *outs[0:3]], [send0, *outs[3:6]]
    m2, m3, d2, d3, wr_b = outs[6:]

    d_near = core(d1)
    d_sum = add(idx, d2, core(d3))
    d_far = across(d_sum)
    if near:
        got = [other(send) for send in sends]
        inward = lambda x: lax.ppermute(x, "heads", [(0, 1), (3, 2)])
        middle = lambda x: lax.ppermute(x, "heads", [(1, 2), (2, 1)])
        outward = lambda x: lax.ppermute(x, "heads", [(1, 0), (2, 3)])
        ones, twos, threes = [None] * 4, [None] * 4, [None] * 4
        ones[0] = add(idx, keeps[0], got[0], after=(d_sum,))
        m_near = core(m1)
        m_sum = add(idx, m2, core(m3), after=(ones[0],))
        m_far = across(m_sum)
        ones[1] = add(idx, keeps[1], got[1], after=(m_sum,))
        twos[0] = add(idx, ones[0], inward(ones[0]), after=(ones[1],))
        before = (twos[0],)
    else:
        m_near = core(m1)
        m_far = across(add(idx, m2, core(m3)))
        before = ()

    own, sib, input_grad = call(
        attn_bwd_kernel,
        shapes(((4, 2, PACK, 128), BF), ((4, 2, PACK, 128), BF), ((SEQ * 2, D), BF)),
        (idx, d0, d_near, d_far, resid, cot0, tok, small, n1)
        + (qkv_a, qkv_b, mix_a, mix_b, wq_a, wq_b, wo_a, wo_b, wr_a, wr_b),
        [
            pltpu.VMEM((ROWS, 384), BF),
            pltpu.VMEM((D, 384), BF),
            pltpu.VMEM((128, D), BF),
            pltpu.VMEM((ROWS, D), F32),
            pltpu.VMEM((8, D), F32),
        ],
        after=before,
        mib=32,
    )

    if near:
        sib = core(sib)
        ones[2] = add(idx, keeps[2], got[2], after=(input_grad,))
        twos[1] = add(idx, ones[1], inward(ones[1]), after=(ones[2],))
        halves = call(merge_kernel, [sds((2, PACK, 128), BF)] * 4, (idx, own, sib), after=(twos[1],))
        halves = [halves[0]] + [flip(halves[j], "heads", j) for j in range(1, 4)]
        threes[0] = add(idx, twos[0], middle(twos[0]), after=(halves[0],))
        ones[3] = add(idx, keeps[3], got[3], after=(threes[0],))
        (output,) = call(
            out_kernel, [sds((SEQ * 2, D), BF)], (idx, resid, m0, m_near, m_far), after=(ones[3],)
        )
        twos[2] = add(idx, ones[2], inward(ones[2]), after=(output,))
        threes[1] = add(idx, twos[1], middle(twos[1]), after=(twos[2],))
        grads = finish(idx, 0, threes[0], outward(threes[0]), after=(threes[1],))
        twos[3] = add(idx, ones[3], inward(ones[3]), after=(grads[0],))
        half, send = call(gather_kernel, [sds((PACK, 128), BF)] * 2, (idx, *halves), after=(twos[3],))
        threes[2] = add(idx, twos[2], middle(twos[2]), after=(half,))
        half = add(idx, half, other(send), after=(threes[2],))
        grads = finish(idx, 1, threes[1], outward(threes[1]), grads, after=(half,))
        half = add(idx, half, across(half), after=(grads[0],))
        threes[3] = add(idx, twos[3], middle(twos[3]), after=(half,))
        grads = finish(idx, 2, threes[2], outward(threes[2]), grads, after=(threes[3],))
        qkv_grad, o_grad, sgrad = call(
            unpack_kernel,
            shapes(((3, 256, 128), F32), ((128, 256), F32), ((8, 256), F32)),
            (idx, half, core(half)),
            after=(grads[0],),
        )
        win_grad, wout_grad = finish(idx, 3, threes[3], outward(threes[3]), grads, after=(sgrad,))
    else:
        (output,) = call(out_kernel, [sds((SEQ * 2, D), BF)], (idx, resid, m0, m_near, m_far))
        keep, send = jnp.stack(keeps), jnp.stack(sends)
        gin = jnp.concatenate([keep[:, :256], send[:, :256]], 1)
        gout = jnp.concatenate([keep[:, 256:], send[:, 256:]], 1).transpose(0, 2, 1)
        win_grad = lax.psum_scatter(gin, "fsdp", scatter_dimension=1, tiled=True)
        wout_grad = lax.psum_scatter(gout, "fsdp", scatter_dimension=2, tiled=True)
        win_grad = lax.psum(win_grad, "heads").astype(F32)
        wout_grad = lax.psum(wout_grad, "heads").astype(F32)
        qkv_grad, o_grad, sgrad = whole_of_packs((own, sib))
        qkv_grad = lax.psum_scatter(qkv_grad, "fsdp", scatter_dimension=1, tiled=True)
        qkv_grad = lax.psum_scatter(qkv_grad, "heads", scatter_dimension=2, tiled=True)
        qkv_grad = lax.psum(qkv_grad, "tensor")
        o_grad = lax.psum_scatter(o_grad, "fsdp", scatter_dimension=1, tiled=True)
        o_grad = lax.psum_scatter(o_grad, "heads", scatter_dimension=0, tiled=True)
        o_grad = lax.psum(o_grad, "tensor")
        sgrad = lax.psum(sgrad, ("fsdp", "heads", "tensor"))
        sgrad = lax.dynamic_slice_in_dim(sgrad, f * gain_one.shape[0], gain_one.shape[0], 1)

    return (
        output,
        input_grad,
        sgrad[4],
        sgrad[5],
        qkv_grad,
        o_grad,
        sgrad[6],
        sgrad[7],
        sgrad[0:4].T,
        win_grad,
        wout_grad,
    )


def solution(mesh):
    placed = (
        P(("fsdp", "heads", "tensor"), None),
        P("fsdp"),
        P("fsdp"),
        P(None, "fsdp", "heads"),
        P("heads", "fsdp"),
        P("fsdp"),
        P("fsdp"),
        P("fsdp", None),
        P(None, "fsdp", "tensor"),
        P(None, "tensor", "fsdp"),
        P(("fsdp", "heads"), None),
        P(("fsdp", "heads", "tensor"), None),
    )
    return jax.shard_map(
        local,
        mesh=mesh,
        in_specs=placed,
        out_specs=(
            P(("fsdp", "heads", "tensor"), None),
            P(("fsdp", "heads", "tensor"), None),
            P("fsdp"),
            P("fsdp"),
            P(None, "fsdp", "heads"),
            P("heads", "fsdp"),
            P("fsdp"),
            P("fsdp"),
            P("fsdp", None),
            P(None, "fsdp", "tensor"),
            P(None, "tensor", "fsdp"),
        ),
        check_vma=False,
    )
```

time: 334 us -> 304 us (0.910)
  waiting for transfers between devices: 178 us -> 143 us
  local copies, waits for them, and re-layouts: 11.2 us -> 22.7 us
  Pallas kernels: 78 us -> 89 us
  other arithmetic: 10.6 us -> 0.08 us
  starting transfers between devices: 54.1 us -> 47.5 us
    ppermute x12, waiting for transfers between devices: 55.4 us -> 17.2 us  [the longest x4 13.2 us: local(): outward = lambda x: lax.ppermute(x, 'heads', [(1, 0), (2, 3)])]
    unnamed x53 -> x73, local copies, waits for them, and re-layouts: 2.74 us -> 21.3 us
    ppermute x43 -> x32, starting transfers between devices: 39.5 us -> 25.1 us  [flip(): return lax.ppermute(x, axis, [(i, i ^ bit) for i in range(n)])]
    pallas_call x9 -> x34, Pallas kernels: 78 us -> 89 us  [the longest x3 42.5 us: moe(): pl.pallas_call(skip(kernel, n_in, len(after)), grid=(n,), out_shape=outs,...]
    ppermute x12, starting transfers between devices: 14.5 us -> 22.4 us  [the longest x4 14.2 us: local(): inward = lambda x: lax.ppermute(x, 'heads', [(0, 1), (3, 2)])]
    convert_element_type x17 -> x0, other arithmetic: 5.32 us -> none  [the longest x1 1.81 us: local(): part = plus(keep[e], other(send[e])).astype(BF)]
    ppermute x43 -> x32, waiting for transfers between devices: 123 us -> 125 us  [flip(): return lax.ppermute(x, axis, [(i, i ^ bit) for i in range(n)])]
  transfers between devices with their start and end apart: 55 -> 44, of which waited for: 25 -> 19; matrix products, arithmetic and copies ran while one was open for 5% -> 0% of each run, Pallas kernels for 15% -> 22%
where the time goes in v2:
time: 304 us; the launch traced here: 303 us
  waiting for transfers between devices  143 us (47%)
  Pallas kernels  89 us (29%)
  starting transfers between devices  47.5 us (16%)
  local copies, waits for them, and re-layouts  22.7 us (7%)
    ppermute x32, waiting for transfers between devices, flip(): return lax.ppermute(x, axis, [(i, i ^ bit) for i in range(n)])  125 us
    pallas_call x3, Pallas kernels, moe(): pl.pallas_call(skip(kernel, n_in, len(after)), grid=(n,), out_shape=outs,...  42.5 us
    pallas_call x27, Pallas kernels, call(): pl.pallas_call(skip(kernel, len(args), len(after)), out_shape=outs, in_sp...  39.8 us
    ppermute x32, starting transfers between devices, flip(): return lax.ppermute(x, axis, [(i, i ^ bit) for i in range(n)])  25.1 us
    unnamed x73, local copies, waits for them, and re-layouts  21.3 us
    ppermute x4, starting transfers between devices, local(): inward = lambda x: lax.ppermute(x, 'heads', [(0, 1), (3, 2)])  14.2 us
    ppermute x4, waiting for transfers between devices, local(): outward = lambda x: lax.ppermute(x, 'heads', [(1, 0), (2, 3)])  13.2 us
    pallas_call x4, Pallas kernels, finish(): pl.pallas_call(skip(finish_kernel, 3, len(into) + len(after)), grid=(1,),...  6.68 us
  transfers between devices with their start and end apart: 44, of which 19 were waited for; matrix products, arithmetic and copies ran while one was open for 0% of the time, Pallas kernels for 22%

profile of v2, /device:TPU:0, one launch (start us, length us, event | category | flops | bytes accessed | tf_op | source)
XLA Modules:
  0.0 303.1 jit_solution(679476923482025004)
XLA Ops:
  9.7 3.0 collective-permute-start.10
  14.2 47.1 %collective-permute-done.refs_2_ = bf16[528,128]{1,0:T(8,128)(2,1)S(1)} collective-permute-done((bf16[528,128]{1,0:T(8,128)(2,1)S(1)}, bf16[528,128]{1,0:T(8,128)(2,1)S(1)}, u32[]{:S(2)}, u32[]{:S(2)}) %collective-permute-start) | collective-permute-done | bytes 135200 | tf_op jit(solution)/shard_map/ppermute | solution.py:461
  63.7 2.5 collective-permute-start.3
  66.3 4.3 %collective-permute-done.6.refs_4_ = bf16[2,528,128]{2,1,0:T(8,128)(2,1)S(1)} collective-permute-done((bf16[2,528,128]{2,1,0:T(8,128)(2,1)S(1)}, bf16[2,528,128]{2,1,0:T(8,128)(2,1)S(1)}, u32[]{:S(2)}, u32[]{:S(2)}) %collective-permute-start.6) | collective-permute-done | bytes 270368 | tf_op jit(solution)/shard_map/ppermute | solution.py:461
  70.6 8.8 %collective-permute-done.3.refs_4_ = bf16[2,528,128]{2,1,0:T(8,128)(2,1)S(1)} collective-permute-done((bf16[2,528,128]{2,1,0:T(8,128)(2,1)S(1)}, bf16[2,528,128]{2,1,0:T(8,128)(2,1)S(1)}, u32[]{:S(2)}, u32[]{:S(2)}) %collective-permute-start.3) | collective-permute-done | bytes 270368 | tf_op jit(solution)/shard_map/ppermute | solution.py:461
  79.5 9.5 %collective-permute-done.1.refs_2_ = bf16[2,528,128]{2,1,0:T(8,128)(2,1)S(1)} collective-permute-done((bf16[2,528,128]{2,1,0:T(8,128)(2,1)S(1)}, bf16[2,528,128]{2,1,0:T(8,128)(2,1)S(1)}, u32[]{:S(2)}, u32[]{:S(2)}) %collective-permute-start.1) | collective-permute-done | bytes 270368 | tf_op jit(solution)/shard_map/ppermute | solution.py:461
  90.6 4.0 %shard_map.207 = (bf16[8,512]{1,0:T(8,128)(2,1)S(1)}, bf16[416,512]{1,0:T(8,128)(2,1)S(1)}, f32[416,512]{1,0:T(8,128)S(1)}, bf16[2,416,384]{2,1,0:T(8,128)(2,1)S...) custom-call(s32[4]{0:T(128)S(1)} %pad_add_fusion.refs_0_, ...), custom_call_target="tpu_custom_call" | custom-call | tf_op jit(solution)/shard_map/pallas_call | solution.py:59
  96.4 4.8 %shard_map.208 = (bf16[416,512]{1,0:T(8,128)(2,1)}, f32[416,512]{1,0:T(8,128)S(1)}, bf16[2,416,384]{2,1,0:T(8,128)(2,1)S(1)}, bf16[2,416,128]{2,1,0:T(8,128)(2,1...) custom-call(s32[4]{0:T(128)S(1)} %pad_add_fusion.refs_0_, ...), custom_call_target="tpu_custom_call" | custom-call | tf_op jit(solution)/shard_map/pallas_call | solution.py:59
  106.1 11.2 %collective-permute-done.12.refs_1_ = bf16[416,512]{1,0:T(8,128)(2,1)} collective-permute-done((bf16[416,512]{1,0:T(8,128)(2,1)}, bf16[416,512]{1,0:T(8,128)(2,1)}, u32[]{:S(2)}, u32[]{:S(2)}) %collective-permute-start.12) | collective-permute-done | bytes 426016 | tf_op jit(solution)/shard_map/ppermute | solution.py:461
  117.5 19.9 %shard_map.209 = (f32[4,512,512]{2,1,0:T(8,128)}, f32[4,512,512]{2,1,0:T(8,128)}, bf16[416,512]{1,0:T(8,128)(2,1)S(1)}, bf16[416,512]{1,0:T(8,128)(2,1)S(1)}, bf...) custom-call(s32[4]{0:T(128)S(1)} %pad_add_fusion.refs_0_, ...), custom_call_target="tpu_custom_call" | custom-call | tf_op jit(solution)/shard_map/pallas_call | solution.py:395
  137.5 6.2 %shard_map.210 = (bf16[512,512]{1,0:T(8,128)(2,1)S(1)}, bf16[512,512]{1,0:T(8,128)(2,1)S(1)}, f32[2,416,512]{2,1,0:T(8,128)S(1)}, f32[2,416,512]{2,1,0:T(8,128)S(1)}, f32[2,416,8]{2,1,0:T(8,128)S(1)}) custom-call(s32[4]{0:T(128)S(1)} %pad_add_fusion.refs_0_, bf16[416,512]{1,0:T(8,128)(2,1)} %collective-permute-done.12.refs_1_, ...), custom_call_target="tpu_custom_call" | custom-call | tf_op jit(solution)/shard_map/pallas_call | solution.py:395
  146.4 16.4 %shard_map.211 = (bf16[512,512]{1,0:T(8,128)(2,1)S(1)}, bf16[512,512]{1,0:T(8,128)(2,1)S(1)}, bf16[512,512]{1,0:T(8,128)(2,1)S(1)}, bf16[512,512]{1,0:T(8,128)(2...) custom-call(s32[4]{0:T(128)S(1)} %pad_add_fusion.refs_0_, ...), custom_call_target="tpu_custom_call" | custom-call | tf_op jit(solution)/shard_map/pallas_call | solution.py:395
  170.6 6.7 %collective-permute-done.22.refs_2_ = bf16[512,512]{1,0:T(8,128)(2,1)S(1)} collective-permute-done((bf16[512,512]{1,0:T(8,128)(2,1)S(1)}, bf16[512,512]{1,0:T(8,128)(2,1)S(1)}, u32[]{:S(2)}, u32[]{:S(2)}) %collective-permute-start.22) | collective-permute-done | bytes 524320 | tf_op jit(solution)/shard_map/ppermute | solution.py:461
  180.4 13.0 %shard_map.217 = (bf16[4,2,528,128]{3,2,1,0:T(8,128)(2,1)S(1)}, bf16[4,2,528,128]{3,2,1,0:T(8,128)(2,1)S(1)}, bf16[394,512]{1,0:T(8,128)(2,1)}) custom-call(s32[4]{0:T(128)S(1)} %pad_add_fusion.refs_0_, bf16[416,512]{1,0:T(8,128)(2,1)S(1)} %get-tuple-element.93.refs_1_, bf16[416,512]{1,0:T(8,128)(2,1)S(1)} %collective-permute-done.24.refs_2_, ...), custom_call_target="tpu_custom_call" | custom-call | tf_op jit(solution)/shard_map/pallas_call | solution.py:59
  194.0 4.0 %collective-permute-start.27 = (bf16[512,512]{1,0:T(8,128)(2,1)S(1)}, bf16[512,512]{1,0:T(8,128)(2,1)S(1)}, u32[]{:S(2)}, u32[]{:S(2)}) collective-permute-start(bf16[512,512]{1,0:T(8,128)(2,1)S(1)} %shard_map.215.refs_3_.refs_1_), channel_id=1, source_target_pairs={{0,4},{12,8},{1,5},{13,9},{2,6},{14,10},{3,7},{15,11},{16,20},{28,... | collective-permute-start | bytes 1572872 | tf_op jit(solution)/shard_map/ppermute | solution.py:578
  200.3 7.8 %collective-permute-done.28.refs_2_ = bf16[512,512]{1,0:T(8,128)(2,1)S(1)} collective-permute-done((bf16[512,512]{1,0:T(8,128)(2,1)S(1)}, bf16[512,512]{1,0:T(8,128)(2,1)S(1)}, u32[]{:S(2)}, u32[]{:S(2)}) %collective-permute-start.28) | collective-permute-done | bytes 524320 | tf_op jit(solution)/shard_map/ppermute | solution.py:461
  209.8 4.1 %collective-permute-start.35 = (bf16[512,512]{1,0:T(8,128)(2,1)S(1)}, bf16[512,512]{1,0:T(8,128)(2,1)S(1)}, u32[]{:S(2)}, u32[]{:S(2)}) collective-permute-start(bf16[512,512]{1,0:T(8,128)(2,1)S(1)} %shard_map.218.refs_3_.refs_1_), channel_id=1, source_target_pairs={{0,4},{12,8},{1,5},{13,9},{2,6},{14,10},{3,7},{15,11},{16,20},{28,... | collective-permute-start | bytes 1572872 | tf_op jit(solution)/shard_map/ppermute | solution.py:578
  219.7 4.1 %collective-permute-start.32 = (bf16[512,512]{1,0:T(8,128)(2,1)S(1)}, bf16[512,512]{1,0:T(8,128)(2,1)S(1)}, u32[]{:S(2)}, u32[]{:S(2)}) collective-permute-start(bf16[512,512]{1,0:T(8,128)(2,1)S(1)} %shard_map.222.refs_5_.refs_1_), channel_id=1, source_target_pairs={{0,4},{12,8},{1,5},{13,9},{2,6},{14,10},{3,7},{15,11},{16,20},{28,... | collective-permute-start | bytes 1572872 | tf_op jit(solution)/shard_map/ppermute | solution.py:578
  229.9 4.9 %collective-permute-start.29 = (bf16[2,528,128]{2,1,0:T(8,128)(2,1)S(1)}, bf16[2,528,128]{2,1,0:T(8,128)(2,1)S(1)}, u32[]{:S(2)}, u32[]{:S(2)}) collective-permute-start(bf16[2,528,128]{2,1,0:T(8,128)(2,1)S(1)} %get-tuple-element.111), channel_id=1, source_target_pairs={{0,4},{4,0},{8,12},{12,8},{1,5},{5,1},{9,13},{13,9},{2,6},{6,2},{1... | collective-permute-start | bytes 811016 | tf_op jit(solution)/shard_map/ppermute | solution.py:461
  234.8 2.6 collective-permute-done.32.refs_2_
  247.3 17.6 %collective-permute-done.30.refs_3_ = bf16[2,528,128]{2,1,0:T(8,128)(2,1)S(1)} collective-permute-done((bf16[2,528,128]{2,1,0:T(8,128)(2,1)S(1)}, bf16[2,528,128]{2,1,0:T(8,128)(2,1)S(1)}, u32[]{:S(2)}, u32[]{:S(2)}) %collective-permute-start.30) | collective-permute-done | bytes 270368 | tf_op jit(solution)/shard_map/ppermute | solution.py:461
  268.3 4.3 %collective-permute-done.36.refs_2_ = bf16[528,128]{1,0:T(8,128)(2,1)S(1)} collective-permute-done((bf16[528,128]{1,0:T(8,128)(2,1)S(1)}, bf16[528,128]{1,0:T(8,128)(2,1)S(1)}, u32[]{:S(2)}, u32[]{:S(2)}) %collective-permute-start.36) | collective-permute-done | bytes 135200 | tf_op jit(solution)/shard_map/ppermute | solution.py:461
  275.4 2.9 collective-permute-done.38.refs_2_
  288.3 13.1 %collective-permute-done.43.refs_2_ = bf16[512,512]{1,0:T(8,128)(2,1)S(1)} collective-permute-done((bf16[512,512]{1,0:T(8,128)(2,1)S(1)}, bf16[512,512]{1,0:T(8,128)(2,1)S(1)}, u32[]{:S(2)}, u32[]{:S(2)}) %collective-permute-start.43) | collective-permute-done | bytes 524320 | tf_op jit(solution)/shard_map/ppermute | solution.py:580
  (178 shorter events, 79.1 us)
Async XLA Ops:
  9.7 107.8 %collective-permute-start.10 = (bf16[4,512,512]{2,1,0:T(8,128)(2,1)S(1)}, bf16[4,512,512]{2,1,0:T(8,128)(2,1)}, u32[]{:S(2)}, u32[]{:S(2)}) collective-permute-start(bf16[4,512,512]{2,1,0:T(8,128)(2,1)S(1)} %shard_map.204.refs_3_.refs_7_), channel_id=1, source_target_pairs={{0,16},{16,0},{1,17},{17,1},{2,18},{18,2},{3,19},{19,3},{4,20},{20... | collective-permute-start | bytes 6291464 | tf_op jit(solution)/shard_map/ppermute | solution.py:461
  12.7 48.5 %collective-permute-start = (bf16[528,128]{1,0:T(8,128)(2,1)S(1)}, bf16[528,128]{1,0:T(8,128)(2,1)S(1)}, u32[]{:S(2)}, u32[]{:S(2)}) collective-permute-start(bf16[528,128]{1,0:T(8,128)(2,1)S(1)} %shard_map.203.refs_3_.refs_1_), channel_id=1, source_target_pairs={{0,16},{16,0},{1,17},{17,1},{2,18},{18,2},{3,19},{19,3},{4,20},{20... | collective-permute-start | bytes 405512 | tf_op jit(solution)/shard_map/ppermute | solution.py:461
  66.2 22.8 %collective-permute-start.1 = (bf16[2,528,128]{2,1,0:T(8,128)(2,1)S(1)}, bf16[2,528,128]{2,1,0:T(8,128)(2,1)S(1)}, u32[]{:S(2)}, u32[]{:S(2)}) collective-permute-start(bf16[2,528,128]{2,1,0:T(8,128)(2,1)S(1)} %shard_map.206.refs_2_), channel_id=1, source_target_pairs={{0,8},{4,12},{8,0},{12,4},{1,9},{5,13},{9,1},{13,5},{2,10},{6,14},... | collective-permute-start | bytes 811016 | tf_op jit(solution)/shard_map/ppermute | solution.py:461
  66.3 22.7 %collective-permute-start.5 = (bf16[2,528,128]{2,1,0:T(8,128)(2,1)S(1)}, bf16[2,528,128]{2,1,0:T(8,128)(2,1)S(1)}, u32[]{:S(2)}, u32[]{:S(2)}) collective-permute-start(bf16[2,528,128]{2,1,0:T(8,128)(2,1)S(1)} %shard_map.206.refs_2_), channel_id=1, source_target_pairs={{0,1},{1,0},{2,3},{3,2},{4,5},{5,4},{6,7},{7,6},{8,9},{9,8},{10,11... | collective-permute-start | bytes 811016 | tf_op jit(solution)/shard_map/ppermute | solution.py:461
  70.6 20.0 %collective-permute-start.7 = (bf16[2,528,128]{2,1,0:T(8,128)(2,1)S(1)}, bf16[2,528,128]{2,1,0:T(8,128)(2,1)S(1)}, u32[]{:S(2)}, u32[]{:S(2)}) collective-permute-start(bf16[2,528,128]{2,1,0:T(8,128)(2,1)S(1)} %collective-permute-done.6.refs_4_), channel_id=1, source_target_pairs={{0,1},{1,0},{2,3},{3,2},{4,5},{5,4},{6,7},{7,6},{8,9},{9,8},{10,11... | collective-permute-start | bytes 811016 | tf_op jit(solution)/shard_map/ppermute | solution.py:461
  79.5 16.9 %collective-permute-start.4 = (bf16[2,528,128]{2,1,0:T(8,128)(2,1)S(1)}, bf16[2,528,128]{2,1,0:T(8,128)(2,1)S(1)}, u32[]{:S(2)}, u32[]{:S(2)}) collective-permute-start(bf16[2,528,128]{2,1,0:T(8,128)(2,1)S(1)} %collective-permute-done.3.refs_4_), channel_id=1, source_target_pairs={{0,1},{1,0},{2,3},{3,2},{4,5},{5,4},{6,7},{7,6},{8,9},{9,8},{10,11... | collective-permute-start | bytes 811016 | tf_op jit(solution)/shard_map/ppermute | solution.py:461
  89.0 17.1 %collective-permute-start.14 = (bf16[416,512]{1,0:T(8,128)(2,1)}, bf16[416,512]{1,0:T(8,128)(2,1)}, u32[]{:S(2)}, u32[]{:S(2)}) collective-permute-start(bf16[416,512]{1,0:T(8,128)(2,1)} %get-tuple-element.75.refs_3_.refs_5_), channel_id=1, source_target_pairs={{0,2},{1,3},{2,0},{3,1},{4,6},{5,7},{6,4},{7,5},{8,10},{9,11},{10,... | collective-permute-start | bytes 1277960 | tf_op jit(solution)/shard_map/ppermute | solution.py:461
  106.1 31.3 %collective-permute-start.15 = (bf16[416,512]{1,0:T(8,128)(2,1)}, bf16[416,512]{1,0:T(8,128)(2,1)}, u32[]{:S(2)}, u32[]{:S(2)}) collective-permute-start(bf16[416,512]{1,0:T(8,128)(2,1)} %collective-permute-done.14.refs_3_), channel_id=1, source_target_pairs={{0,1},{1,0},{2,3},{3,2},{4,5},{5,4},{6,7},{7,6},{8,9},{9,8},{10,11... | collective-permute-start | bytes 1277960 | tf_op jit(solution)/shard_map/ppermute | solution.py:461
  117.3 20.2 %collective-permute-start.13 = (bf16[416,512]{1,0:T(8,128)(2,1)}, bf16[416,512]{1,0:T(8,128)(2,1)}, u32[]{:S(2)}, u32[]{:S(2)}) collective-permute-start(bf16[416,512]{1,0:T(8,128)(2,1)} %collective-permute-done.12.refs_1_), channel_id=1, source_target_pairs={{0,1},{1,0},{2,3},{3,2},{4,5},{5,4},{6,7},{7,6},{8,9},{9,8},{10,11... | collective-permute-start | bytes 1277960 | tf_op jit(solution)/shard_map/ppermute | solution.py:461
  144.9 20.4 %collective-permute-start.17 = (bf16[512,512]{1,0:T(8,128)(2,1)S(1)}, bf16[512,512]{1,0:T(8,128)(2,1)S(1)}, u32[]{:S(2)}, u32[]{:S(2)}) collective-permute-start(bf16[512,512]{1,0:T(8,128)(2,1)S(1)} %get-tuple-element.86), channel_id=1, source_target_pairs={{0,16},{16,0},{1,17},{17,1},{2,18},{18,2},{3,19},{19,3},{4,20},{20... | collective-permute-start | bytes 1572872 | tf_op jit(solution)/shard_map/ppermute | solution.py:461
  193.4 20.5 %collective-permute-start.26 = (bf16[4,2,528,128]{3,2,1,0:T(8,128)(2,1)S(1)}, bf16[4,2,528,128]{3,2,1,0:T(8,128)(2,1)S(1)}, u32[]{:S(2)}, u32[]{:S(2)}) collective-permute-start(bf16[4,2,528,128]{3,2,1,0:T(8,128)(2,1)S(1)} %get-tuple-element.106), channel_id=1, source_target_pairs={{0,1},{1,0},{2,3},{3,2},{4,5},{5,4},{6,7},{7,6},{8,9},{9,8},{10,11... | collective-permute-start | bytes 3244040 | tf_op jit(solution)/shard_map/ppermute | solution.py:461
  198.0 18.0 %collective-permute-start.23 = (bf16[512,512]{1,0:T(8,128)(2,1)S(1)}, bf16[512,512]{1,0:T(8,128)(2,1)S(1)}, u32[]{:S(2)}, u32[]{:S(2)}) collective-permute-start(bf16[512,512]{1,0:T(8,128)(2,1)S(1)} %shard_map.216.refs_19_.refs_1_), channel_id=1, source_target_pairs={{4,8},{8,4},{5,9},{9,5},{6,10},{10,6},{7,11},{11,7},{20,24},{24,20... | collective-permute-start | bytes 1572872 | tf_op jit(solution)/shard_map/ppermute | solution.py:579
  198.7 20.3 %collective-permute-start.20 = (bf16[512,512]{1,0:T(8,128)(2,1)S(1)}, bf16[512,512]{1,0:T(8,128)(2,1)S(1)}, u32[]{:S(2)}, u32[]{:S(2)}) collective-permute-start(bf16[512,512]{1,0:T(8,128)(2,1)S(1)} %get-tuple-element.90), channel_id=1, source_target_pairs={{0,16},{16,0},{1,17},{17,1},{2,18},{18,2},{3,19},{19,3},{4,20},{20... | collective-permute-start | bytes 1572872 | tf_op jit(solution)/shard_map/ppermute | solution.py:461
  209.8 17.7 %collective-permute-start.35 = (bf16[512,512]{1,0:T(8,128)(2,1)S(1)}, bf16[512,512]{1,0:T(8,128)(2,1)S(1)}, u32[]{:S(2)}, u32[]{:S(2)}) collective-permute-start(bf16[512,512]{1,0:T(8,128)(2,1)S(1)} %shard_map.218.refs_3_.refs_1_), channel_id=1, source_target_pairs={{0,4},{12,8},{1,5},{13,9},{2,6},{14,10},{3,7},{15,11},{16,20},{28,... | collective-permute-start | bytes 1572872 | tf_op jit(solution)/shard_map/ppermute | solution.py:578
  216.0 18.8 %collective-permute-start.34 = (bf16[512,512]{1,0:T(8,128)(2,1)S(1)}, bf16[512,512]{1,0:T(8,128)(2,1)S(1)}, u32[]{:S(2)}, u32[]{:S(2)}) collective-permute-start(bf16[512,512]{1,0:T(8,128)(2,1)S(1)} %shard_map.219.refs_3_.refs_1_), channel_id=1, source_target_pairs={{4,8},{8,4},{5,9},{9,5},{6,10},{10,6},{7,11},{11,7},{20,24},{24,20... | collective-permute-start | bytes 1572872 | tf_op jit(solution)/shard_map/ppermute | solution.py:579
  219.7 17.7 %collective-permute-start.32 = (bf16[512,512]{1,0:T(8,128)(2,1)S(1)}, bf16[512,512]{1,0:T(8,128)(2,1)S(1)}, u32[]{:S(2)}, u32[]{:S(2)}) collective-permute-start(bf16[512,512]{1,0:T(8,128)(2,1)S(1)} %shard_map.222.refs_5_.refs_1_), channel_id=1, source_target_pairs={{0,4},{12,8},{1,5},{13,9},{2,6},{14,10},{3,7},{15,11},{16,20},{28,... | collective-permute-start | bytes 1572872 | tf_op jit(solution)/shard_map/ppermute | solution.py:578
  223.8 16.8 %collective-permute-start.33 = (bf16[512,512]{1,0:T(8,128)(2,1)S(1)}, bf16[512,512]{1,0:T(8,128)(2,1)S(1)}, u32[]{:S(2)}, u32[]{:S(2)}) collective-permute-start(bf16[512,512]{1,0:T(8,128)(2,1)S(1)} %shard_map.221.refs_3_.refs_1_), channel_id=1, source_target_pairs={{4,0},{8,12},{5,1},{9,13},{6,2},{10,14},{7,3},{11,15},{20,16},{24,... | collective-permute-start | bytes 1572872 | tf_op jit(solution)/shard_map/ppermute | solution.py:580
  229.2 36.4 %collective-permute-start.37 = (bf16[512,512]{1,0:T(8,128)(2,1)S(1)}, bf16[512,512]{1,0:T(8,128)(2,1)S(1)}, u32[]{:S(2)}, u32[]{:S(2)}) collective-permute-start(bf16[512,512]{1,0:T(8,128)(2,1)S(1)} %shard_map.224.refs_3_.refs_1_), channel_id=1, source_target_pairs={{4,8},{8,4},{5,9},{9,5},{6,10},{10,6},{7,11},{11,7},{20,24},{24,20... | collective-permute-start | bytes 1572872 | tf_op jit(solution)/shard_map/ppermute | solution.py:579
  229.9 16.7 %collective-permute-start.29 = (bf16[2,528,128]{2,1,0:T(8,128)(2,1)S(1)}, bf16[2,528,128]{2,1,0:T(8,128)(2,1)S(1)}, u32[]{:S(2)}, u32[]{:S(2)}) collective-permute-start(bf16[2,528,128]{2,1,0:T(8,128)(2,1)S(1)} %get-tuple-element.111), channel_id=1, source_target_pairs={{0,4},{4,0},{8,12},{12,8},{1,5},{5,1},{9,13},{13,9},{2,6},{6,2},{1... | collective-permute-start | bytes 811016 | tf_op jit(solution)/shard_map/ppermute | solution.py:461
  234.8 30.1 %collective-permute-start.30 = (bf16[2,528,128]{2,1,0:T(8,128)(2,1)S(1)}, bf16[2,528,128]{2,1,0:T(8,128)(2,1)S(1)}, u32[]{:S(2)}, u32[]{:S(2)}) collective-permute-start(bf16[2,528,128]{2,1,0:T(8,128)(2,1)S(1)} %get-tuple-element.112), channel_id=1, source_target_pairs={{0,8},{4,12},{8,0},{12,4},{1,9},{5,13},{9,1},{13,5},{2,10},{6,14},... | collective-permute-start | bytes 811016 | tf_op jit(solution)/shard_map/ppermute | solution.py:461
  237.4 27.5 %collective-permute-start.31 = (bf16[2,528,128]{2,1,0:T(8,128)(2,1)S(1)}, bf16[2,528,128]{2,1,0:T(8,128)(2,1)S(1)}, u32[]{:S(2)}, u32[]{:S(2)}) collective-permute-start(bf16[2,528,128]{2,1,0:T(8,128)(2,1)S(1)} %get-tuple-element.113), channel_id=1, source_target_pairs={{0,12},{4,8},{8,4},{12,0},{1,13},{5,9},{9,5},{13,1},{2,14},{6,10},... | collective-permute-start | bytes 811016 | tf_op jit(solution)/shard_map/ppermute | solution.py:461
  240.6 33.1 %collective-permute-start.39 = (bf16[512,512]{1,0:T(8,128)(2,1)S(1)}, bf16[512,512]{1,0:T(8,128)(2,1)S(1)}, u32[]{:S(2)}, u32[]{:S(2)}) collective-permute-start(bf16[512,512]{1,0:T(8,128)(2,1)S(1)} %shard_map.225.refs_3_.refs_1_), channel_id=1, source_target_pairs={{4,0},{8,12},{5,1},{9,13},{6,2},{10,14},{7,3},{11,15},{20,16},{24,... | collective-permute-start | bytes 1572872 | tf_op jit(solution)/shard_map/ppermute | solution.py:580
  246.6 33.9 %collective-permute-start.42 = (bf16[512,512]{1,0:T(8,128)(2,1)S(1)}, bf16[512,512]{1,0:T(8,128)(2,1)S(1)}, u32[]{:S(2)}, u32[]{:S(2)}) collective-permute-start(bf16[512,512]{1,0:T(8,128)(2,1)S(1)} %shard_map.227.refs_5_.refs_1_), channel_id=1, source_target_pairs={{4,8},{8,4},{5,9},{9,5},{6,10},{10,6},{7,11},{11,7},{20,24},{24,20... | collective-permute-start | bytes 1572872 | tf_op jit(solution)/shard_map/ppermute | solution.py:579
  281.2 20.2 %collective-permute-start.43 = (bf16[512,512]{1,0:T(8,128)(2,1)S(1)}, bf16[512,512]{1,0:T(8,128)(2,1)S(1)}, u32[]{:S(2)}, u32[]{:S(2)}) collective-permute-start(bf16[512,512]{1,0:T(8,128)(2,1)S(1)} %shard_map.233.refs_5_.refs_1_), channel_id=1, source_target_pairs={{4,0},{8,12},{5,1},{9,13},{6,2},{10,14},{7,3},{11,15},{20,16},{24,... | collective-permute-start | bytes 1572872 | tf_op jit(solution)/shard_map/ppermute | solution.py:580
  (56 other events, 498.5 us)
